TPU v7x, 128 devices: a whole 4x4x4 slice. The times are simulated.
128 devices in a mesh: row: 32 (over x, z_hi, y), col: 4 (over z_lo, core).
Axes of the slice: x: 4, y: 4, z: 4 (z_hi: 2, z_lo: 2; z = z_hi * 2 + z_lo), core: 2. Of those that a mesh axis runs over, the one named last changes fastest.
Arguments:
- pair_act: bfloat16 [768, 4096, 128], P('row', 'col'), may hold values from -6 to 6
- pair_cot: bfloat16 [768, 4096, 128], P('row', 'col'), may hold values from -6 to 6
- pair_mask: int32 [768, 4096], P('row', 'col'), may hold values 0 or 1
- pair_norm_gain: float32 [128], replicated, may hold values from 0.25 to 1.75
- pair_norm_bias: float32 [128], replicated, may hold values from -3 to 3
- proj_weight: bfloat16 [128, 128], replicated, may hold values from -0.5 to 0.5
- left_weight: bfloat16 [384, 128], replicated, may hold values from -0.3125 to 0.3125
- right_weight: bfloat16 [384, 128], replicated, may hold values from -0.3125 to 0.3125
Outputs:
- pair_activation_gradient: bfloat16 [768, 4096, 128], P('row', 'col')
- row_single_grad: float32 [768, 384], P('row')
- col_single_grad: float32 [4096, 384], P(('col', 'row'))
- weight_grad: float32 [128, 128], replicated
- gain_grad: float32 [128], replicated
- bias_grad: float32 [128], replicated
All inputs are finite; a program needn't handle non-finite values. No bound on the sum of `pair_mask` on one device may be relied on, other than what follows from the above.
Results may differ from a plain program's by a relative error of at most 0.0031.
Values sent between devices are 32-bit elements; how exact they have to be, the bound alone decides.
No kernel may reach another device: no remote copies, remote signals or barrier semaphores. Data moves between devices by JAX's collectives and lax.ppermute only.
A program may use at most 128 MiB of HBM per device.

v0:
```python
import jax
import jax.numpy as jnp
from jax import lax
from jax.sharding import PartitionSpec as P


def shards(
    pair_act,
    pair_cot,
    pair_mask,
    pair_norm_gain,
    pair_norm_bias,
    proj_weight,
    left_weight,
    right_weight,
):
    pair_input = pair_act.astype(jnp.float32)
    pair_mean = jnp.mean(pair_input, axis=-1, keepdims=True)
    var = jnp.mean((pair_input - pair_mean) * (pair_input - pair_mean), axis=-1, keepdims=True)
    inverse_deviation = lax.rsqrt(var + 1e-05)
    standardized_input = (pair_input - pair_mean) * inverse_deviation
    normalized_pair = (standardized_input * pair_norm_gain + pair_norm_bias).astype(jnp.bfloat16)
    dz = pair_cot * pair_mask.astype(jnp.bfloat16)[..., None]
    normalized_gradient = jnp.einsum(
        "rnd,ed->rne", dz, proj_weight, preferred_element_type=jnp.float32
    )
    centered_gradient = normalized_gradient * pair_norm_gain
    first_term = jnp.mean(centered_gradient, axis=-1, keepdims=True)
    second_term = jnp.mean(centered_gradient * standardized_input, axis=-1, keepdims=True)
    pair_activation_gradient = (
        inverse_deviation * (centered_gradient - first_term - standardized_input * second_term)
    ).astype(jnp.bfloat16)
    weight_part = jnp.einsum("rnc,rnd->cd", normalized_pair, dz, preferred_element_type=jnp.float32)
    gain_partial = jnp.sum(normalized_gradient * standardized_input, axis=(0, 1))
    bias_part = jnp.sum(normalized_gradient, axis=(0, 1))
    rows_all = pair_act.shape[0] * lax.axis_size("row")
    cols_all = pair_act.shape[1] * lax.axis_size("col")
    scale = 1.0 / jnp.sqrt(jnp.float32(rows_all) * jnp.float32(cols_all))
    dzf = dz.astype(jnp.float32)
    row_part = jnp.sum(dzf, axis=1)
    row_total = lax.psum(row_part, "col")
    left_float = left_weight.astype(jnp.float32)
    right_float = right_weight.astype(jnp.float32)
    row_single_grad = jnp.einsum(
        "rc,sc->rs", row_total, left_float, precision=lax.Precision.HIGHEST
    )
    col_part = jnp.sum(dzf, axis=0)
    weight_sum, gain_sum, bias_sum = lax.psum(
        (weight_part, gain_partial, bias_part), ("row", "col")
    )
    col_total = lax.psum_scatter(col_part, "row", scatter_dimension=0, tiled=True)
    col_single_grad = jnp.einsum(
        "rc,sc->rs", col_total, right_float, precision=lax.Precision.HIGHEST
    )
    return (
        pair_activation_gradient,
        row_single_grad,
        col_single_grad,
        weight_sum * scale,
        gain_sum * scale,
        bias_sum * scale,
    )


def solution(mesh):
    in_specs = (
        P("row", "col", None),
        P("row", "col", None),
        P("row", "col"),
        P(),
        P(),
        P(),
        P(),
        P(),
    )
    out_specs = (P("row", "col", None), P("row", None), P(("col", "row"), None), P(), P(), P())
    return jax.shard_map(shards, mesh=mesh, in_specs=in_specs, out_specs=out_specs, check_vma=False)
```

profile of v0, /device:TPU:0, one launch (start us, length us, event | category | flops | bytes accessed | tf_op | source)
XLA Modules:
  0.0 242.2 jit_solution(8406952761624154523)
XLA Ops:
  8.0 0.0 copy-start
  8.0 0.0 copy-start.3
  8.0 0.0 copy-start.5
  8.0 0.0 copy-start.7
  8.0 0.0 all-reduce.3.cloned.1.call-start
  8.1 0.0 copy-start.1
  8.1 0.0 copy-start.2
  8.1 4.7 %convert_reduce_fusion.2 = f32[24,1024]{1,0:T(8,128)S(1)} fusion(bf16[24,1024,128]{2,1,0:T(8,128)(2,1)} %param.8), kind=kLoop, calls=%fused_computation.3 | loop fusion | flops 6266880 | bytes 6389760 | tf_op jit(solution)/shard_map/reduce_sum | solution.py:18
  12.8 10.0 %fusion.13 = f32[24,1024]{1,0:T(8,128)S(1)} fusion(bf16[24,1024,128]{2,1,0:T(8,128)(2,1)} %param.8, f32[24,1024]{1,0:T(8,128)S(1)} %broadcast_multiply_fusion.2), kind=kLoop, calls=%fused_computation.17 | loop fusion | flops 12558336 | bytes 6488064 | tf_op jit(solution)/shard_map/reduce_sum | solution.py:19
  22.8 0.0 copy-done.3
  22.8 0.0 copy-done.5
  22.8 0.0 copy-done.7
  22.8 0.0 copy-done.1
  22.9 0.0 copy-done.2
  22.9 0.0 copy-start.6
  22.9 15.5 %fusion.25 = f32[128,128]{1,0:T(8,128)} fusion(bf16[24,1024,128]{2,1,0:T(8,128)(2,1)S(1)} %copy-done.2, bf16[24,1024]{1,0:T(8,128)(2,1)S(1)} %convert_element_type.18, bf16[24,1024,128]{2,1,0:T(8,128)(2,1)S(1)} %copy-done.1, f32[128]{0:T(128)S(1)} %copy-done.7, f32[128]{0:T(128)S(1)} %copy-done.5, f32[24,1024]{1,0:T(8,128)S(1)} %add_rsqrt_fusion, ...), kind=kOutput, calls=%fused_computation.29 | convolution fusion | flops 827326464 | bytes 12895232 | tf_op jit(solution)/shard_map/rnc,rnd->cd/dot_general | solution.py:33
  38.4 0.0 all-reduce.3.cloned.1.call-update
  38.4 0.0 reduce-scatter.2.cloned.1.call-start
  38.5 8.1 %convert_reduce_fusion = (f32[1024,128]{1,0:T(8,128)}, f32[24,128]{1,0:T(8,128)S(1)}) fusion(bf16[24,1024,128]{2,1,0:T(8,128)(2,1)} %param.9, bf16[24,1024]{1,0:T(8,128)(2,1)S(1)} %convert_element_type.18), kind=kLoop, calls=%fused_computation | loop fusion | flops 12448768 | bytes 6877184 | tf_op jit(solution)/shard_map/reduce_sum | solution.py:47
  46.6 0.0 reduce-scatter.2.cloned.1.call-update
  46.6 0.0 copy-done.6
  46.6 0.0 copy-start.4
  46.6 20.8 %fusion.12 = (f32[128]{0:T(128)S(1)}, f32[24,1024]{1,0:T(8,128)S(1)}, f32[24,1024]{1,0:T(8,128)S(1)}, f32[128]{0:T(128)S(1)}, f32[24,1024,128]{2,1,0:T(8,128)}) fusion(bf16[24,1024,128]{2,1,0:T(8,128)(2,1)} %param.8, f32[24,1024]{1,0:T(8,128)S(1)} %add_rsqrt_fusion, f32[24,1024]{1,0:T(8,128)S(1)} %broadcast_multiply_fusion.2, f32[128]{0:T(128)S(1)} %copy-done.5, ...), kind=kOutput, calls=%fused_computation.16 | convolution fusion | flops 839859968 | bytes 25642496 | tf_op jit(solution)/shard_map/rnd,ed->rne/dot_general | solution.py:24
  67.4 12.1 %psum.28 = f32[24,128]{1,0:T(8,128)S(1)} all-reduce(f32[24,128]{1,0:T(8,128)S(1)} %get-tuple-element.11), channel_id=1, replica_groups=mesh['row'=32,'col'=4] {'col'}, use_global_device_ids=true, to_apply=%region_5.0 | all-reduce | flops 3072 | bytes 24576 | tf_op jit(solution)/shard_map/psum | solution.py:41
  79.5 67.5 %all-reduce = (f32[128]{0:T(128)S(1)}, f32[128]{0:T(128)S(1)}) all-reduce(f32[128]{0:T(128)S(1)} %get-tuple-element.6, f32[128]{0:T(128)S(1)} %get-tuple-element.9), channel_id=1, replica_groups=mesh['row'=32,'col'=4] {'row','col'}, use_global_device_ids=true, to_apply=%region_10.0 | all-reduce | flops 256 | bytes 2048 | tf_op jit(solution)/shard_map/psum | solution.py:48
  147.0 0.5 broadcast_multiply_fusion.4
  147.5 0.8 fusion.31
  148.4 18.8 %fusion.9 = bf16[24,1024,128]{2,1,0:T(8,128)(2,1)} fusion(bf16[24,1024,128]{2,1,0:T(8,128)(2,1)} %param.8, f32[24,1024,128]{2,1,0:T(8,128)} %get-tuple-element.14, f32[24,1024]{1,0:T(8,128)S(1)} %get-tuple-element.15, f32[24,1024]{1,0:T(8,128)S(1)} %get-tuple-element.16, f32[128]{0:T(128)S(1)} %copy-done.5, f32[24,1024]{1,0:T(8,128)S(1)} %add_rsqrt_fusion, ...), kind=kLoop, calls=%fused_computation.13 | loop fusion | flops 28311552 | bytes 25559552 | tf_op jit(solution)/shard_map/convert_element_type | solution.py:32
  167.2 10.2 %all-reduce.3.cloned.1.call-done = f32[128,128]{1,0:T(8,128)} async-done(((f32[128,128]{1,0:T(8,128)}), f32[128,128]{1,0:T(8,128)}) %all-reduce.3.cloned.1.call-update) | async-done | bytes 65552 | tf_op jit(solution)/shard_map/psum | solution.py:48
  177.4 1.5 broadcast_multiply_fusion.3
  178.9 54.3 %reduce-scatter.2.cloned.1.call-done = f32[32,128]{1,0:T(8,128)} async-done(((f32[1024,128]{1,0:T(8,128)}), f32[32,128]{1,0:T(8,128)}) %reduce-scatter.2.cloned.1.call-update) | async-done | bytes 16400 | tf_op jit(solution)/shard_map/reduce_scatter | solution.py:51
  233.2 1.6 fusion.32
  (6 shorter events, 0.1 us)
Async XLA Ops:
  8.0 225.2 %copy-start = (bf16[384,128]{1,0:T(8,128)(2,1)S(1)}, bf16[384,128]{1,0:T(8,128)(2,1)}, u32[]{:S(2)}) copy-start(bf16[384,128]{1,0:T(8,128)(2,1)} %param.15) | copy-start | bytes 294916
  8.0 14.8 %copy-start.3 = (s32[24,1024]{1,0:T(8,128)S(1)}, s32[24,1024]{1,0:T(8,128)}, u32[]{:S(2)}) copy-start(s32[24,1024]{1,0:T(8,128)} %param.10) | copy-start | bytes 294916
  8.0 14.8 %copy-start.5 = (f32[128]{0:T(128)S(1)}, f32[128]{0:T(128)}, u32[]{:S(2)}) copy-start(f32[128]{0:T(128)} %param.11) | copy-start | bytes 1540
  8.0 14.8 %copy-start.7 = (f32[128]{0:T(128)S(1)}, f32[128]{0:T(128)}, u32[]{:S(2)}) copy-start(f32[128]{0:T(128)} %param.12) | copy-start | bytes 1540
  8.0 169.3 %all-reduce.3.cloned.1.call-start = ((), (), s32[]{:S(2)}) async-start(), calls=%async_computation.2 | async-start | bytes 131072 | tf_op jit(solution)/shard_map/psum | solution.py:48
  8.1 14.8 %copy-start.1 = (bf16[24,1024,128]{2,1,0:T(8,128)(2,1)S(1)}, bf16[24,1024,128]{2,1,0:T(8,128)(2,1)}, u32[]{:S(2)}) copy-start(bf16[24,1024,128]{2,1,0:T(8,128)(2,1)} %param.8) | copy-start | bytes 18874372
  8.1 14.8 %copy-start.2 = (bf16[24,1024,128]{2,1,0:T(8,128)(2,1)S(1)}, bf16[24,1024,128]{2,1,0:T(8,128)(2,1)}, u32[]{:S(2)}) copy-start(bf16[24,1024,128]{2,1,0:T(8,128)(2,1)} %param.9) | copy-start | bytes 18874372
  22.9 23.7 %copy-start.6 = (bf16[128,128]{1,0:T(8,128)(2,1)S(1)}, bf16[128,128]{1,0:T(8,128)(2,1)}, u32[]{:S(2)}) copy-start(bf16[128,128]{1,0:T(8,128)(2,1)} %param.13) | copy-start | bytes 98308
  38.4 194.8 %reduce-scatter.2.cloned.1.call-start = ((), (), s32[]{:S(2)}) async-start(), calls=%async_computation.1 | async-start | bytes 540672 | tf_op jit(solution)/shard_map/reduce_scatter | solution.py:51
  46.6 101.0 %copy-start.4 = (bf16[384,128]{1,0:T(8,128)(2,1)S(1)}, bf16[384,128]{1,0:T(8,128)(2,1)}, u32[]{:S(2)}) copy-start(bf16[384,128]{1,0:T(8,128)(2,1)} %param.14) | copy-start | bytes 294916
Sparse Core Ops, SparseCore 0:
  38.5 138.8 all-reduce.2
Sparse Core Ops, SparseCore 1:
  46.7 186.4 reduce-scatter.1
where the time goes:
time: 243 us; the launch traced here: 242 us
  blocking collectives  79.6 us (33%)
  waiting for transfers between devices  64.5 us (27%)
  other arithmetic  43.6 us (18%)
  matrix products  38.7 us (16%)
  between operations  15.6 us (6%)
    psum x1, blocking collectives, shards(): lax.psum((weight_part, gain_partial, bias_part), ('row', 'col'))  67.5 us
    reduce_scatter x1, waiting for transfers between devices, shards(): lax.psum_scatter(col_part, 'row', scatter_dimension=0, tiled=True)  54.3 us
    dot_general x1, matrix products, shards(): jnp.einsum('rnd,ed->rne', dz, proj_weight, preferred_element_type=jnp.flo...  20.8 us
    convert_element_type x1, other arithmetic, shards(): pair_activation_gradient = (inverse_deviation * (centered_gradient - firs...  18.8 us
    dot_general x1, matrix products, shards(): jnp.einsum('rnc,rnd->cd', normalized_pair, dz, preferred_element_type=jnp...  15.5 us
    psum x1, blocking collectives, shards(): row_total = lax.psum(row_part, 'col')  12.1 us
    psum x1, waiting for transfers between devices, shards(): lax.psum((weight_part, gain_partial, bias_part), ('row', 'col'))  10.2 us
    reduce_sum x1, other arithmetic, shards(): jnp.mean((pair_input - pair_mean) * (pair_input - pair_mean), axis=-1, ke...  9.97 us
  transfers between devices with their start and end apart: 2, of which 2 were waited for; matrix products, arithmetic and copies ran while one was open for 21% of the time, Pallas kernels for 0%

commit v1 on v0

v1 whole, which is shorter than its diff:
```python
import functools

import jax
import jax.numpy as jnp
from jax import lax
from jax.experimental import pallas as pl
from jax.experimental.pallas import tpu as pltpu
from jax.sharding import PartitionSpec as P

EPS = 1e-05
NT = (((1,), (1,)), ((), ()))
COLS = 128
SUB = 32
WIDE = 256
VMEM = 58 << 20


def sums_kernel(x_hbm, cot_hbm, mask_ref, g_ref, send_ref, keep_ref, xv, cv, mf, mv, cc, sems):
    rows, n, c = x_hbm.shape
    chunks = n // COLS
    quarters = COLS // SUB
    bands = rows // quarters
    k = rows * SUB

    def copies(j):
        cols = pl.ds(pl.multiple_of(j * COLS, COLS), COLS)
        return (
            pltpu.make_async_copy(x_hbm.at[:, cols], xv.at[j], sems.at[0, j]),
            pltpu.make_async_copy(cot_hbm.at[:, cols], cv.at[j], sems.at[1, j]),
        )

    for j in range(chunks):
        for copy in copies(j):
            copy.start()
    lane = lax.broadcasted_iota(jnp.int32, (bands, COLS), 1) // SUB
    for j in range(chunks):
        mf[j * rows:(j + 1) * rows, :] = mask_ref[:, j * COLS:(j + 1) * COLS].astype(jnp.float32)
        strips = [mf[pl.ds(j * rows + i, bands, stride=quarters), :] for i in range(quarters)]
        for q in range(quarters):
            mixed = jnp.zeros((bands, COLS), jnp.float32)
            for i in range(quarters):
                shift = ((i - q) * SUB) % COLS
                moved = strips[i] if shift == 0 else pltpu.roll(strips[i], shift, 1)
                mixed = jnp.where(lane == i, moved, mixed)
            mv[q, j, :bands, :] = mixed
    g_ref[...] = jnp.zeros_like(g_ref)
    wide_lane = lax.broadcasted_iota(jnp.int32, (SUB, k), 1)
    wide_sub = lax.broadcasted_iota(jnp.int32, (SUB, k), 0)
    pattern = jnp.concatenate(
        [jnp.where(wide_sub == wide_lane // SUB, 1.0, 0.0), jnp.where(wide_sub == wide_lane % SUB, 1.0, 0.0)], axis=0
    ).astype(jnp.bfloat16)
    r = lax.axis_index("row")
    core = lax.axis_index("col") % 2

    @pl.loop(0, chunks)
    def _(j):
        for copy in copies(j):
            copy.wait()
        total = jnp.zeros((c + SUB, c), jnp.float32)
        columns = []
        for q in range(quarters):
            cot = cv[j, :, q * SUB:(q + 1) * SUB, :].reshape(k, c)
            masks = [mv[q, j, b:b + 1, :] for b in range(bands)]
            parts = []
            for b in range(bands):
                block = xv[j, b * quarters:(b + 1) * quarters, q * SUB:(q + 1) * SUB, :]
                xt = block.reshape(COLS, c).T.astype(jnp.float32)
                xc = xt - jnp.sum(xt, axis=0, keepdims=True) * (1.0 / c)
                var = jnp.sum(xc * xc, axis=0, keepdims=True) * (1.0 / c)
                parts.append((xc * (lax.rsqrt(var + EPS) * masks[b])).astype(jnp.bfloat16))
            mrow = jnp.concatenate([jnp.broadcast_to(m, (16, COLS)).astype(jnp.bfloat16) for m in masks], axis=1)
            lhs = [jnp.concatenate(parts, axis=1)] + [pattern[16 * t:16 * t + 16] * mrow for t in range(4)]
            out = jnp.dot(jnp.concatenate(lhs, axis=0), cot, preferred_element_type=jnp.float32)
            total += out[:c + SUB]
            columns.append(out[c + SUB:])
        for q in range(quarters):
            d = (j * quarters + q) ^ r
            x1, x0, z, y1, y0 = [(d >> s) & 1 for s in (4, 3, 2, 1, 0)]
            px, py = x0 ^ x1, y0 ^ y1
            s4 = jnp.where(core == 0, px, py)
            s3 = jnp.where(core == 0, py, px)
            s2 = jnp.where(core == 0, x1, y1)
            s1 = jnp.where(core == 0, y1, x1)
            off = pl.multiple_of((s4 * 16 + s3 * 8 + s2 * 4 + s1 * 2 + z) * SUB, SUB)
            cc[pl.ds(off, SUB), :] = columns[q]
        g_ref[:c] += total[:c]
        g_ref[c + 8:] += total[c:c + rows]

    keep_ref[...] = cc[:n // 2]
    send_ref[...] = cc[n // 2:]
    g_ref[c:c + 8] = jnp.broadcast_to(jnp.sum(g_ref[c + 8:], axis=0, keepdims=True), (8, c))


def sums(x, cot, mask):
    rows, n, c = x.shape
    vm = pl.BlockSpec(memory_space=pltpu.VMEM)
    hbm = pl.BlockSpec(memory_space=pl.ANY)
    return pl.pallas_call(
        sums_kernel,
        in_specs=[hbm, hbm, vm],
        out_specs=[vm] * 3,
        out_shape=[
            jax.ShapeDtypeStruct((c + 8 + rows, c), jnp.float32),
            jax.ShapeDtypeStruct((n // 2, c), jnp.float32),
            jax.ShapeDtypeStruct((n // 2, c), jnp.float32),
        ],
        scratch_shapes=[
            pltpu.VMEM((n // COLS, rows, COLS, c), jnp.bfloat16),
            pltpu.VMEM((n // COLS, rows, COLS, c), jnp.bfloat16),
            pltpu.VMEM((rows * (n // COLS), COLS), jnp.float32),
            pltpu.VMEM((COLS // SUB, n // COLS, 8, COLS), jnp.float32),
            pltpu.VMEM((n, c), jnp.float32),
            pltpu.SemaphoreType.DMA((2, n // COLS)),
        ],
        compiler_params=pltpu.CompilerParams(vmem_limit_bytes=VMEM),
        name="sums",
    )(x, cot, mask)


def grad_kernel(x_ref, cot_ref, mask_ref, gain_ref, w_ref, out_ref, wt):
    rows, cols, c = x_ref.shape

    @pl.when(pl.program_id(0) == 0)
    def _():
        wg = w_ref[...].astype(jnp.float32) * jnp.broadcast_to(gain_ref[...], (c, c)).T
        wg = wg - jnp.mean(wg, axis=0, keepdims=True)
        high = wg.astype(jnp.bfloat16)
        wt[:c] = high
        wt[c:] = (wg - high.astype(jnp.float32)).astype(jnp.bfloat16)

    p = rows * cols
    both = lax.dot_general(wt[...], cot_ref[...].reshape(p, c), NT, preferred_element_type=jnp.float32)
    dc = both[:c] + both[c:]
    mask = jnp.concatenate([mask_ref[i:i + 1, :].astype(jnp.float32) for i in range(rows)], axis=1)
    xt = x_ref[...].reshape(p, c).T.astype(jnp.float32)
    xc = xt - jnp.sum(xt, axis=0, keepdims=True) * (1.0 / c)
    var = jnp.sum(xc * xc, axis=0, keepdims=True) * (1.0 / c)
    q = jnp.sum(xc * dc, axis=0, keepdims=True) * (1.0 / c)
    rstd = lax.rsqrt(var + EPS)
    masked = rstd * mask
    out = (dc * masked - xc * (masked * rstd * rstd * q)).astype(jnp.bfloat16)
    out_ref[...] = out.T.reshape(rows, cols, c)


def grads(x, cot, mask, gain, w):
    rows, n, c = x.shape
    wide = pl.BlockSpec((rows, WIDE, c), lambda j: (0, j, 0))
    return pl.pallas_call(
        grad_kernel,
        grid=(n // WIDE,),
        in_specs=[
            wide,
            wide,
            pl.BlockSpec((rows, WIDE), lambda j: (0, j)),
            pl.BlockSpec((1, c), lambda j: (0, 0)),
            pl.BlockSpec((c, c), lambda j: (0, 0)),
        ],
        out_specs=wide,
        out_shape=jax.ShapeDtypeStruct((rows, n, c), jnp.bfloat16),
        scratch_shapes=[pltpu.VMEM((2 * c, c), jnp.bfloat16)],
        compiler_params=pltpu.CompilerParams(vmem_limit_bytes=VMEM),
        cost_estimate=pl.CostEstimate(flops=6 * rows * n * c * c, bytes_accessed=6 * rows * n * c, transcendentals=0),
        name="activation_gradient",
    )(x, cot, mask, gain.reshape(1, c), w)


def tail_kernel(g_ref, gain_ref, bias_ref, w_ref, weight_ref, gains_ref, biases_ref, *, scale):
    c = w_ref.shape[0]
    g = g_ref[:c]
    total = g_ref[c:c + 1]
    w = w_ref[...].astype(jnp.float32)
    gain = jnp.broadcast_to(gain_ref[...], (c, c)).T
    bias = jnp.broadcast_to(bias_ref[...], (c, c)).T
    weight_ref[...] = (gain * g + bias * total) * scale
    gains_ref[...] = jnp.sum((w * g).T, axis=0, keepdims=True) * scale
    biases_ref[...] = jnp.sum((w * total).T, axis=0, keepdims=True) * scale


def tail(g, gain, bias, w, scale):
    c = w.shape[0]
    vm = pl.BlockSpec(memory_space=pltpu.VMEM)
    weight, gains, biases = pl.pallas_call(
        functools.partial(tail_kernel, scale=scale),
        in_specs=[vm] * 4,
        out_specs=[vm] * 3,
        out_shape=[
            jax.ShapeDtypeStruct((c, c), jnp.float32),
            jax.ShapeDtypeStruct((1, c), jnp.float32),
            jax.ShapeDtypeStruct((1, c), jnp.float32),
        ],
        name="parameter_gradients",
    )(g, gain.reshape(1, c), bias.reshape(1, c), w)
    return weight, gains.reshape(c), biases.reshape(c)


def flipped(i, move):
    axis, bits = move
    x, z, y, core = i >> 5, ((i >> 4) & 1) * 2 + ((i >> 1) & 1), (i >> 2) & 3, i & 1
    x ^= bits if axis == "x" else 0
    y ^= bits if axis == "y" else 0
    z ^= bits if axis == "z" else 0
    core ^= bits if axis == "core" else 0
    return (((x * 2 + (z >> 1)) * 4 + y) * 2 + (z & 1)) * 2 + core


def exchange(value, move, other=None):
    moves = (move, other or move)
    pairs = [(i, flipped(i, moves[i & 1])) for i in range(128)]
    return lax.ppermute(value, ("row", "col"), pairs)


ORDER = (
    (("x", 1), ("y", 1)),
    (("y", 1), ("x", 1)),
    (("x", 3), ("y", 3)),
    (("y", 3), ("x", 3)),
)


def shards(pair_act, pair_cot, pair_mask, gain, bias, w, left_weight, right_weight):
    rows, n, c = pair_act.shape
    pairs = rows * lax.axis_size("row") * n * lax.axis_size("col")
    scale = 1.0 / float(pairs) ** 0.5
    g, send, keep = sums(pair_act, pair_cot, pair_mask)
    activation_gradient = grads(pair_act, pair_cot, pair_mask, gain, w)

    g = g + exchange(g, ("core", 1))
    g = g + exchange(g, ("z", 1))
    row_total = g[c + 8:]
    g = g[:c + 8]
    size = n // 2
    for move, other in ORDER:
        got = exchange(send, move, other)
        size //= 2
        send = keep[size:] + got[size:]
        keep = keep[:size] + got[:size]
        g = g + exchange(g, move, other)
    g = g + exchange(g, ("z", 3))
    col_total = keep + exchange(send, ("z", 2))

    row_single_grad = jnp.einsum(
        "rc,sc->rs", row_total, left_weight.astype(jnp.float32), precision=lax.Precision.HIGHEST
    )
    col_single_grad = jnp.einsum(
        "rc,sc->rs", col_total, right_weight.astype(jnp.float32), precision=lax.Precision.HIGHEST
    )
    weight_grad, gain_grad, bias_grad = tail(g, gain, bias, w, scale)
    return activation_gradient, row_single_grad, col_single_grad, weight_grad, gain_grad, bias_grad


def solution(mesh):
    in_specs = (
        P("row", "col", None),
        P("row", "col", None),
        P("row", "col"),
        P(),
        P(),
        P(),
        P(),
        P(),
    )
    out_specs = (P("row", "col", None), P("row", None), P(("col", "row"), None), P(), P(), P())
    return jax.shard_map(shards, mesh=mesh, in_specs=in_specs, out_specs=out_specs, check_vma=False)
```

time: 243 us -> 60.7 us (0.25)
  blocking collectives: 79.6 us -> 0 us
  waiting for transfers between devices: 64.5 us -> 8.88 us
  other arithmetic: 43.6 us -> 2.63 us
  matrix products: 38.7 us -> 1.68 us
  starting transfers between devices: 0.08 us -> 23.5 us
  Pallas kernels: 0 us -> 23.1 us
  between operations: 15.6 us -> 0.7 us
    psum x2 -> x0, blocking collectives: 79.6 us -> none  [the longest x1 67.5 us: shards(): lax.psum((weight_part, gain_partial, bias_part), ('row', 'col'))]
    reduce_scatter x1 -> x0, waiting for transfers between devices: 54.3 us -> none  [shards(): lax.psum_scatter(col_part, 'row', scatter_dimension=0, tiled=True)]
    dot_general x4 -> x2, matrix products: 38.7 us -> 1.68 us  [the longest x1 0.84 us: shards(): jnp.einsum('rc,sc->rs', col_total, right_weight.astype(jnp.float32), prec...]
    ppermute x0 -> x12, starting transfers between devices: none -> 23.5 us  [exchange(): return lax.ppermute(value, ('row', 'col'), pairs)]
    pallas_call x0 -> x3, Pallas kernels: none -> 23.1 us  [the longest x1 11.4 us: grads(): pl.pallas_call(grad_kernel, grid=(n // WIDE,), in_specs=[wide, wide, pl.B...]
    reduce_sum x3 -> x0, other arithmetic: 22.7 us -> none  [the longest x1 9.97 us: shards(): jnp.mean((pair_input - pair_mean) * (pair_input - pair_mean), axis=-1, ke...]
    convert_element_type x2 -> x0, other arithmetic: 18.8 us -> none  [the longest x1 18.8 us: shards(): pair_activation_gradient = (inverse_deviation * (centered_gradient - firs...]
    psum x1 -> x0, waiting for transfers between devices: 10.2 us -> none  [shards(): lax.psum((weight_part, gain_partial, bias_part), ('row', 'col'))]
  transfers between devices with their start and end apart: 2 -> 12, of which waited for: 2 -> 7; matrix products, arithmetic and copies ran while one was open for 21% -> 6% of each run, Pallas kernels for 0% -> 19%
where the time goes in v1:
time: 60.7 us; the launch traced here: 60.5 us
  starting transfers between devices  23.5 us (39%)
  Pallas kernels  23.1 us (38%)
  waiting for transfers between devices  8.88 us (15%)
  other arithmetic  2.63 us (4%)
  matrix products  1.68 us (3%)
  between operations  0.7 us (1%)
    ppermute x12, starting transfers between devices, exchange(): return lax.ppermute(value, ('row', 'col'), pairs)  23.5 us
    pallas_call x1, Pallas kernels, grads(): pl.pallas_call(grad_kernel, grid=(n // WIDE,), in_specs=[wide, wide, pl.B...  11.4 us
    pallas_call x1, Pallas kernels, sums(): pl.pallas_call(sums_kernel, in_specs=[hbm, hbm, vm], out_specs=[vm] * 3,...  10.1 us
    ppermute x12, waiting for transfers between devices, exchange(): return lax.ppermute(value, ('row', 'col'), pairs)  8.88 us
    pallas_call x1, Pallas kernels, tail(): pl.pallas_call(functools.partial(tail_kernel, scale=scale), in_specs=[vm]...  1.64 us
  transfers between devices with their start and end apart: 12, of which 7 were waited for; matrix products, arithmetic and copies ran while one was open for 6% of the time, Pallas kernels for 19%

profile of v1, /device:TPU:0, one launch (start us, length us, event | category | flops | bytes accessed | tf_op | source)
XLA Modules:
  0.0 60.5 jit_solution(16664786539353813660)
XLA Ops:
  0.6 0.0 copy-start
  0.6 10.1 %sums.1 = (f32[160,128]{1,0:T(8,128)}, f32[512,128]{1,0:T(8,128)}, f32[512,128]{1,0:T(8,128)}) custom-call(bf16[24,1024,128]{2,1,0:T(8,128)(2,1)} %x_hbm.1, bf16[24,1024,128]{2,1,0:T(8,128)(2,1)} %cot_hbm.1, s32[24,1024]{1,0:T(8,128)} %mask_ref.3), custom_call_target="tpu_custom_call" | custom-call | tf_op jit(solution)/shard_map/sums/pallas_call | solution.py:98
  10.7 1.7 %collective-permute-start.2 = (f32[512,128]{1,0:T(8,128)}, f32[512,128]{1,0:T(8,128)S(1)}, u32[]{:S(2)}, u32[]{:S(2)}) collective-permute-start(f32[512,128]{1,0:T(8,128)} %get-tuple-element.14), channel_id=1, source_target_pairs={{0,32},{1,5},{2,34},{3,7},{4,36},{5,1},{6,38},{7,3},{8,40},{9,13},... | collective-permute-start | bytes 786440 | tf_op jit(solution)/shard_map/ppermute | solution.py:209
  12.4 1.5 %collective-permute-done = f32[160,128]{1,0:T(8,128)S(1)} collective-permute-done((f32[160,128]{1,0:T(8,128)}, f32[160,128]{1,0:T(8,128)S(1)}, u32[]{:S(2)}, u32[]{:S(2)}) %collective-permute-start) | collective-permute-done | bytes 81952 | tf_op jit(solution)/shard_map/ppermute | solution.py:209
  13.9 0.9 %add.48 = f32[160,128]{1,0:T(8,128)S(1)} add(f32[160,128]{1,0:T(8,128)} %get-tuple-element.12, f32[160,128]{1,0:T(8,128)S(1)} %collective-permute-done) | non-fusion elementwise | flops 20480 | bytes 245760 | tf_op jit(solution)/shard_map/add | solution.py:227
  14.8 2.0 %collective-permute-start.1 = (f32[160,128]{1,0:T(8,128)S(1)}, f32[160,128]{1,0:T(8,128)S(1)}, u32[]{:S(2)}, u32[]{:S(2)}) collective-permute-start(f32[160,128]{1,0:T(8,128)S(1)} %add.48), channel_id=1, source_target_pairs={{0,2},{1,3},{2,0},{3,1},{4,6},{5,7},{6,4},{7,5},{8,10},{9,11},{10,... | collective-permute-start | bytes 245768 | tf_op jit(solution)/shard_map/ppermute | solution.py:209
  16.8 2.8 %collective-permute-done.1 = f32[160,128]{1,0:T(8,128)S(1)} collective-permute-done((f32[160,128]{1,0:T(8,128)S(1)}, f32[160,128]{1,0:T(8,128)S(1)}, u32[]{:S(2)}, u32[]{:S(2)}) %collective-permute-start.1) | collective-permute-done | bytes 81952 | tf_op jit(solution)/shard_map/ppermute | solution.py:209
  19.6 1.1 %collective-permute-start.7 = (f32[136,128]{1,0:T(8,128)S(1)}, f32[136,128]{1,0:T(8,128)S(1)}, u32[]{:S(2)}, u32[]{:S(2)}) collective-permute-start(f32[136,128]{1,0:T(8,128)S(1)} %slice.87), channel_id=1, source_target_pairs={{0,32},{1,5},{2,34},{3,7},{4,36},{5,1},{6,38},{7,3},{8,40},{9,13},... | collective-permute-start | bytes 208904 | tf_op jit(solution)/shard_map/ppermute | solution.py:209
  20.6 0.0 collective-permute-done.2
  20.6 1.0 %slice_add_fusion.1 = (f32[256,128]{1,0:T(8,128)S(1)}, f32[256,128]{1,0:T(8,128)S(1)}) fusion(f32[512,128]{1,0:T(8,128)S(1)} %collective-permute-done.2, f32[512,128]{1,0:T(8,128)} %get-tuple-element.13), kind=kLoop, calls=%fused_computation.1 | loop fusion | flops 65536 | bytes 786432 | tf_op jit(solution)/shard_map/add | solution.py:236
  21.6 1.2 %collective-permute-start.3 = (f32[256,128]{1,0:T(8,128)S(1)}, f32[256,128]{1,0:T(8,128)S(1)}, u32[]{:S(2)}, u32[]{:S(2)}) collective-permute-start(f32[256,128]{1,0:T(8,128)S(1)} %get-tuple-element.19), channel_id=1, source_target_pairs={{0,4},{1,33},{2,6},{3,35},{4,0},{5,37},{6,2},{7,39},{8,12},{9,41},... | collective-permute-start | bytes 393224 | tf_op jit(solution)/shard_map/ppermute | solution.py:209
  22.8 1.1 %collective-permute-done.7 = f32[136,128]{1,0:T(8,128)S(1)} collective-permute-done((f32[136,128]{1,0:T(8,128)S(1)}, f32[136,128]{1,0:T(8,128)S(1)}, u32[]{:S(2)}, u32[]{:S(2)}) %collective-permute-start.7) | collective-permute-done | bytes 69664 | tf_op jit(solution)/shard_map/ppermute | solution.py:209
  24.0 2.4 %collective-permute-start.8 = (f32[136,128]{1,0:T(8,128)S(1)}, f32[136,128]{1,0:T(8,128)S(1)}, u32[]{:S(2)}, u32[]{:S(2)}) collective-permute-start(f32[136,128]{1,0:T(8,128)S(1)} %slice_add_fusion.8), channel_id=1, source_target_pairs={{0,4},{1,33},{2,6},{3,35},{4,0},{5,37},{6,2},{7,39},{8,12},{9,41},... | collective-permute-start | bytes 208904 | tf_op jit(solution)/shard_map/ppermute | solution.py:209
  26.4 0.3 collective-permute-done.3
  26.7 2.4 %collective-permute-start.4 = (f32[128,128]{1,0:T(8,128)S(1)}, f32[128,128]{1,0:T(8,128)S(1)}, u32[]{:S(2)}, u32[]{:S(2)}) collective-permute-start(f32[128,128]{1,0:T(8,128)S(1)} %get-tuple-element.21), channel_id=1, source_target_pairs={{0,96},{1,13},{2,98},{3,15},{4,100},{5,9},{6,102},{7,11},{8,104},{... | collective-permute-start | bytes 196616 | tf_op jit(solution)/shard_map/ppermute | solution.py:209
  29.1 0.0 collective-permute-done.8
  29.1 1.6 %collective-permute-start.9 = (f32[136,128]{1,0:T(8,128)S(1)}, f32[136,128]{1,0:T(8,128)S(1)}, u32[]{:S(2)}, u32[]{:S(2)}) collective-permute-start(f32[136,128]{1,0:T(8,128)S(1)} %add.60), channel_id=1, source_target_pairs={{0,96},{1,13},{2,98},{3,15},{4,100},{5,9},{6,102},{7,11},{8,104},{... | collective-permute-start | bytes 208904 | tf_op jit(solution)/shard_map/ppermute | solution.py:209
  30.7 1.5 %collective-permute-done.4 = f32[128,128]{1,0:T(8,128)S(1)} collective-permute-done((f32[128,128]{1,0:T(8,128)S(1)}, f32[128,128]{1,0:T(8,128)S(1)}, u32[]{:S(2)}, u32[]{:S(2)}) %collective-permute-start.4) | collective-permute-done | bytes 65568 | tf_op jit(solution)/shard_map/ppermute | solution.py:209
  32.3 2.6 %collective-permute-start.5 = (f32[64,128]{1,0:T(8,128)S(1)}, f32[64,128]{1,0:T(8,128)S(1)}, u32[]{:S(2)}, u32[]{:S(2)}) collective-permute-start(f32[64,128]{1,0:T(8,128)S(1)} %get-tuple-element.23), channel_id=1, source_target_pairs={{0,12},{1,97},{2,14},{3,99},{4,8},{5,101},{6,10},{7,103},{8,4},{9,... | collective-permute-start | bytes 98312 | tf_op jit(solution)/shard_map/ppermute | solution.py:209
  34.9 11.4 %activation_gradient.1 = bf16[24,1024,128]{2,1,0:T(8,128)(2,1)} custom-call(bf16[24,1024,128]{2,1,0:T(8,128)(2,1)} %x_hbm.1, bf16[24,1024,128]{2,1,0:T(8,128)(2,1)} %cot_hbm.1, s32[24,1024]{1,0:T(8,128)} %mask_ref.3, f32[1,128]{1,0:T(1,128)} %bitcast.6, bf16[128,128]{1,0:T(8,128)(2,1)} %w_ref.3), custom_call_target="tpu_custom_call" | custom-call | flops 2415919104 | bytes 18874368 | tf_op jit(solution)/shard_map/activation_gradient/pallas_call | solution.py:148
  46.3 0.0 collective-permute-done.9
  46.3 0.7 %collective-permute-start.10 = (f32[136,128]{1,0:T(8,128)S(1)}, f32[136,128]{1,0:T(8,128)S(1)}, u32[]{:S(2)}, u32[]{:S(2)}) collective-permute-start(f32[136,128]{1,0:T(8,128)S(1)} %add.61), channel_id=1, source_target_pairs={{0,12},{1,97},{2,14},{3,99},{4,8},{5,101},{6,10},{7,103},{8,4},{9,... | collective-permute-start | bytes 208904 | tf_op jit(solution)/shard_map/ppermute | solution.py:209
  47.1 0.0 collective-permute-done.5
  47.1 3.8 %collective-permute-start.6 = (f32[32,128]{1,0:T(8,128)S(1)}, f32[32,128]{1,0:T(8,128)S(1)}, u32[]{:S(2)}, u32[]{:S(2)}) collective-permute-start(f32[32,128]{1,0:T(8,128)S(1)} %slice_add_fusion.6), channel_id=1, source_target_pairs={{0,16},{1,17},{2,18},{3,19},{4,20},{5,21},{6,22},{7,23},{8,24},{9,... | collective-permute-start | bytes 49160 | tf_op jit(solution)/shard_map/ppermute | solution.py:209
  50.9 0.8 %fusion.4 = f32[24,384]{1,0:T(8,128)} fusion(bf16[384,128]{1,0:T(8,128)(2,1)S(1)} %copy-done.1, f32[160,128]{1,0:T(8,128)S(1)} %add.49), kind=kOutput, calls=%fused_computation.11 | convolution fusion | flops 14155776 | bytes 147456 | tf_op jit(solution)/shard_map/rc,sc->rs/dot_general | solution.py:241
  51.7 0.2 collective-permute-done.10
  51.9 4.0 %collective-permute-start.11 = (f32[136,128]{1,0:T(8,128)S(1)}, f32[136,128]{1,0:T(8,128)S(1)}, u32[]{:S(2)}, u32[]{:S(2)}) collective-permute-start(f32[136,128]{1,0:T(8,128)S(1)} %add.62), channel_id=1, source_target_pairs={{0,18},{1,19},{2,16},{3,17},{4,22},{5,23},{6,20},{7,21},{8,26},{9,... | collective-permute-start | bytes 208904 | tf_op jit(solution)/shard_map/ppermute | solution.py:209
  55.9 0.0 collective-permute-done.6
  55.9 0.8 %fusion.1 = f32[32,384]{1,0:T(8,128)} fusion(bf16[384,128]{1,0:T(8,128)(2,1)S(1)} %copy-done, f32[32,128]{1,0:T(8,128)S(1)} %collective-permute-done.6, f32[64,128]{1,0:T(8,128)S(1)} %collective-permute-done.5, f32[64,128]{1,0:T(8,128)S(1)} %get-tuple-element.22), kind=kOutput, calls=%fused_computation.9 | convolution fusion | flops 18882560 | bytes 196608 | tf_op jit(solution)/shard_map/rc,sc->rs/dot_general | solution.py:244
  56.7 1.4 %collective-permute-done.11 = f32[136,128]{1,0:T(8,128)S(1)} collective-permute-done((f32[136,128]{1,0:T(8,128)S(1)}, f32[136,128]{1,0:T(8,128)S(1)}, u32[]{:S(2)}, u32[]{:S(2)}) %collective-permute-start.11) | collective-permute-done | bytes 69664 | tf_op jit(solution)/shard_map/ppermute | solution.py:209
  58.2 0.7 %add.63.g_ref = f32[136,128]{1,0:T(8,128)} add(f32[136,128]{1,0:T(8,128)S(1)} %add.62, f32[136,128]{1,0:T(8,128)S(1)} %collective-permute-done.11) | non-fusion elementwise | flops 17408 | bytes 208896 | tf_op jit(solution)/shard_map/add | solution.py:238
  58.8 1.6 %parameter_gradients.1 = (f32[128,128]{1,0:T(8,128)}, f32[1,128]{1,0:T(1,128)}, f32[1,128]{1,0:T(1,128)}) custom-call(f32[136,128]{1,0:T(8,128)} %add.63.g_ref, f32[1,128]{1,0:T(1,128)} %bitcast.7, f32[1,128]{1,0:T(1,128)} %bitcast.8, bf16[128,128]{1,0:T(8,128)(2,1)} %w_ref.3), custom_call_target="tpu_custom_call" | custom-call | tf_op jit(solution)/shard_map/parameter_gradients/pallas_call | solution.py:182
  (13 shorter events, 0.1 us)
Async XLA Ops:
  0.6 55.3 %copy-start = (bf16[384,128]{1,0:T(8,128)(2,1)S(1)}, bf16[384,128]{1,0:T(8,128)(2,1)}, u32[]{:S(2)}) copy-start(bf16[384,128]{1,0:T(8,128)(2,1)} %param.15) | copy-start | bytes 294916
  10.7 9.9 %collective-permute-start.2 = (f32[512,128]{1,0:T(8,128)}, f32[512,128]{1,0:T(8,128)S(1)}, u32[]{:S(2)}, u32[]{:S(2)}) collective-permute-start(f32[512,128]{1,0:T(8,128)} %get-tuple-element.14), channel_id=1, source_target_pairs={{0,32},{1,5},{2,34},{3,7},{4,36},{5,1},{6,38},{7,3},{8,40},{9,13},... | collective-permute-start | bytes 786440 | tf_op jit(solution)/shard_map/ppermute | solution.py:209
  12.4 1.5 %collective-permute-start = (f32[160,128]{1,0:T(8,128)}, f32[160,128]{1,0:T(8,128)S(1)}, u32[]{:S(2)}, u32[]{:S(2)}) collective-permute-start(f32[160,128]{1,0:T(8,128)} %get-tuple-element.12), channel_id=1, source_target_pairs={{0,1},{1,0},{2,3},{3,2},{4,5},{5,4},{6,7},{7,6},{8,9},{9,8},{10,11... | collective-permute-start | bytes 245768 | tf_op jit(solution)/shard_map/ppermute | solution.py:209
  14.8 4.8 %collective-permute-start.1 = (f32[160,128]{1,0:T(8,128)S(1)}, f32[160,128]{1,0:T(8,128)S(1)}, u32[]{:S(2)}, u32[]{:S(2)}) collective-permute-start(f32[160,128]{1,0:T(8,128)S(1)} %add.48), channel_id=1, source_target_pairs={{0,2},{1,3},{2,0},{3,1},{4,6},{5,7},{6,4},{7,5},{8,10},{9,11},{10,... | collective-permute-start | bytes 245768 | tf_op jit(solution)/shard_map/ppermute | solution.py:209
  19.6 4.4 %collective-permute-start.7 = (f32[136,128]{1,0:T(8,128)S(1)}, f32[136,128]{1,0:T(8,128)S(1)}, u32[]{:S(2)}, u32[]{:S(2)}) collective-permute-start(f32[136,128]{1,0:T(8,128)S(1)} %slice.87), channel_id=1, source_target_pairs={{0,32},{1,5},{2,34},{3,7},{4,36},{5,1},{6,38},{7,3},{8,40},{9,13},... | collective-permute-start | bytes 208904 | tf_op jit(solution)/shard_map/ppermute | solution.py:209
  21.6 5.0 %collective-permute-start.3 = (f32[256,128]{1,0:T(8,128)S(1)}, f32[256,128]{1,0:T(8,128)S(1)}, u32[]{:S(2)}, u32[]{:S(2)}) collective-permute-start(f32[256,128]{1,0:T(8,128)S(1)} %get-tuple-element.19), channel_id=1, source_target_pairs={{0,4},{1,33},{2,6},{3,35},{4,0},{5,37},{6,2},{7,39},{8,12},{9,41},... | collective-permute-start | bytes 393224 | tf_op jit(solution)/shard_map/ppermute | solution.py:209
  24.0 5.1 %collective-permute-start.8 = (f32[136,128]{1,0:T(8,128)S(1)}, f32[136,128]{1,0:T(8,128)S(1)}, u32[]{:S(2)}, u32[]{:S(2)}) collective-permute-start(f32[136,128]{1,0:T(8,128)S(1)} %slice_add_fusion.8), channel_id=1, source_target_pairs={{0,4},{1,33},{2,6},{3,35},{4,0},{5,37},{6,2},{7,39},{8,12},{9,41},... | collective-permute-start | bytes 208904 | tf_op jit(solution)/shard_map/ppermute | solution.py:209
  26.7 5.6 %collective-permute-start.4 = (f32[128,128]{1,0:T(8,128)S(1)}, f32[128,128]{1,0:T(8,128)S(1)}, u32[]{:S(2)}, u32[]{:S(2)}) collective-permute-start(f32[128,128]{1,0:T(8,128)S(1)} %get-tuple-element.21), channel_id=1, source_target_pairs={{0,96},{1,13},{2,98},{3,15},{4,100},{5,9},{6,102},{7,11},{8,104},{... | collective-permute-start | bytes 196616 | tf_op jit(solution)/shard_map/ppermute | solution.py:209
  29.1 17.2 %collective-permute-start.9 = (f32[136,128]{1,0:T(8,128)S(1)}, f32[136,128]{1,0:T(8,128)S(1)}, u32[]{:S(2)}, u32[]{:S(2)}) collective-permute-start(f32[136,128]{1,0:T(8,128)S(1)} %add.60), channel_id=1, source_target_pairs={{0,96},{1,13},{2,98},{3,15},{4,100},{5,9},{6,102},{7,11},{8,104},{... | collective-permute-start | bytes 208904 | tf_op jit(solution)/shard_map/ppermute | solution.py:209
  32.3 14.8 %collective-permute-start.5 = (f32[64,128]{1,0:T(8,128)S(1)}, f32[64,128]{1,0:T(8,128)S(1)}, u32[]{:S(2)}, u32[]{:S(2)}) collective-permute-start(f32[64,128]{1,0:T(8,128)S(1)} %get-tuple-element.23), channel_id=1, source_target_pairs={{0,12},{1,97},{2,14},{3,99},{4,8},{5,101},{6,10},{7,103},{8,4},{9,... | collective-permute-start | bytes 98312 | tf_op jit(solution)/shard_map/ppermute | solution.py:209
  34.9 15.9 %copy-start.1 = (bf16[384,128]{1,0:T(8,128)(2,1)S(1)}, bf16[384,128]{1,0:T(8,128)(2,1)}, u32[]{:S(2)}) copy-start(bf16[384,128]{1,0:T(8,128)(2,1)} %param.14) | copy-start | bytes 294916
  46.3 5.6 %collective-permute-start.10 = (f32[136,128]{1,0:T(8,128)S(1)}, f32[136,128]{1,0:T(8,128)S(1)}, u32[]{:S(2)}, u32[]{:S(2)}) collective-permute-start(f32[136,128]{1,0:T(8,128)S(1)} %add.61), channel_id=1, source_target_pairs={{0,12},{1,97},{2,14},{3,99},{4,8},{5,101},{6,10},{7,103},{8,4},{9,... | collective-permute-start | bytes 208904 | tf_op jit(solution)/shard_map/ppermute | solution.py:209
  47.1 8.8 %collective-permute-start.6 = (f32[32,128]{1,0:T(8,128)S(1)}, f32[32,128]{1,0:T(8,128)S(1)}, u32[]{:S(2)}, u32[]{:S(2)}) collective-permute-start(f32[32,128]{1,0:T(8,128)S(1)} %slice_add_fusion.6), channel_id=1, source_target_pairs={{0,16},{1,17},{2,18},{3,19},{4,20},{5,21},{6,22},{7,23},{8,24},{9,... | collective-permute-start | bytes 49160 | tf_op jit(solution)/shard_map/ppermute | solution.py:209
  51.9 6.2 %collective-permute-start.11 = (f32[136,128]{1,0:T(8,128)S(1)}, f32[136,128]{1,0:T(8,128)S(1)}, u32[]{:S(2)}, u32[]{:S(2)}) collective-permute-start(f32[136,128]{1,0:T(8,128)S(1)} %add.62), channel_id=1, source_target_pairs={{0,18},{1,19},{2,16},{3,17},{4,22},{5,23},{6,20},{7,21},{8,26},{9,... | collective-permute-start | bytes 208904 | tf_op jit(solution)/shard_map/ppermute | solution.py:209

commit v2 on v1

v2 whole, which is shorter than its diff:
```python
import functools

import jax
import jax.numpy as jnp
from jax import lax
from jax.experimental import pallas as pl
from jax.experimental.pallas import tpu as pltpu
from jax.sharding import PartitionSpec as P

EPS = 1e-05
NT = (((1,), (1,)), ((), ()))
COLS = 128
SUB = 32
VMEM = 38 << 20
SMALL = 4 << 20


def sums_kernel(
    x_hbm, cot_hbm, mask_ref, first_ref, keep_ref, row_ref, xv, cv, mf, mv, cc, sems
):
    rows, n, c = x_hbm.shape
    chunks = n // COLS
    quarters = COLS // SUB
    bands = rows // quarters
    k = rows * SUB

    def copies(j):
        cols = pl.ds(pl.multiple_of(j * COLS, COLS), COLS)
        return (
            pltpu.make_async_copy(x_hbm.at[:, cols], xv.at[j], sems.at[0, j]),
            pltpu.make_async_copy(cot_hbm.at[:, cols], cv.at[j], sems.at[1, j]),
        )

    for j in range(chunks):
        for copy in copies(j):
            copy.start()
    lane = lax.broadcasted_iota(jnp.int32, (bands, COLS), 1) // SUB
    for j in range(chunks):
        mf[j * rows:(j + 1) * rows, :] = mask_ref[:, j * COLS:(j + 1) * COLS].astype(jnp.float32)
        strips = [mf[pl.ds(j * rows + i, bands, stride=quarters), :] for i in range(quarters)]
        for q in range(quarters):
            mixed = jnp.zeros((bands, COLS), jnp.float32)
            for i in range(quarters):
                shift = ((i - q) * SUB) % COLS
                moved = strips[i] if shift == 0 else pltpu.roll(strips[i], shift, 1)
                mixed = jnp.where(lane == i, moved, mixed)
            mv[q, j, :bands, :] = mixed
    first_ref[:c + 8] = jnp.zeros((c + 8, c), jnp.float32)
    row_ref[...] = jnp.zeros_like(row_ref)
    wide_lane = lax.broadcasted_iota(jnp.int32, (SUB, k), 1)
    wide_sub = lax.broadcasted_iota(jnp.int32, (SUB, k), 0)
    pattern = jnp.concatenate(
        [jnp.where(wide_sub == wide_lane // SUB, 1.0, 0.0), jnp.where(wide_sub == wide_lane % SUB, 1.0, 0.0)], axis=0
    ).astype(jnp.bfloat16)
    r = lax.axis_index("row")
    core = lax.axis_index("col") % 2

    @pl.loop(0, chunks)
    def _(j):
        for copy in copies(j):
            copy.wait()
        total = jnp.zeros((c + SUB, c), jnp.float32)
        columns = []
        for q in range(quarters):
            cot = cv[j, :, q * SUB:(q + 1) * SUB, :].reshape(k, c)
            masks = [mv[q, j, b:b + 1, :] for b in range(bands)]
            parts = []
            for b in range(bands):
                block = xv[j, b * quarters:(b + 1) * quarters, q * SUB:(q + 1) * SUB, :]
                xt = block.reshape(COLS, c).T.astype(jnp.float32)
                xc = xt - jnp.sum(xt, axis=0, keepdims=True) * (1.0 / c)
                var = jnp.sum(xc * xc, axis=0, keepdims=True) * (1.0 / c)
                parts.append((xc * (lax.rsqrt(var + EPS) * masks[b])).astype(jnp.bfloat16))
            mrow = jnp.concatenate([jnp.broadcast_to(m, (16, COLS)).astype(jnp.bfloat16) for m in masks], axis=1)
            lhs = [jnp.concatenate(parts, axis=1)] + [pattern[16 * t:16 * t + 16] * mrow for t in range(4)]
            out = jnp.dot(jnp.concatenate(lhs, axis=0), cot, preferred_element_type=jnp.float32)
            total += out[:c + SUB]
            columns.append(out[c + SUB:])
        for q in range(quarters):
            d = (j * quarters + q) ^ r
            x1, x0, z, y1, y0 = [(d >> s) & 1 for s in (4, 3, 2, 1, 0)]
            px, py = x0 ^ x1, y0 ^ y1
            s4 = jnp.where(core == 0, px, py)
            s3 = jnp.where(core == 0, py, px)
            s2 = jnp.where(core == 0, x1, y1)
            s1 = jnp.where(core == 0, y1, x1)
            off = pl.multiple_of((s4 * 16 + s3 * 8 + s2 * 4 + s1 * 2 + z) * SUB, SUB)
            cc[pl.ds(off, SUB), :] = columns[q]
        first_ref[:c] += total[:c]
        row_ref[...] += total[c:c + rows]

    keep_ref[...] = cc[:n // 2]
    first_ref[c + 8:] = cc[n // 2:]
    first_ref[c:c + 8] = jnp.broadcast_to(jnp.sum(row_ref[...], axis=0, keepdims=True), (8, c))


def sums(x, cot, mask):
    rows, n, c = x.shape
    vm = pl.BlockSpec(memory_space=pltpu.VMEM)
    hbm = pl.BlockSpec(memory_space=pl.ANY)
    chunks = jax.ShapeDtypeStruct((n // COLS, rows, COLS, c), jnp.bfloat16)
    return pl.pallas_call(
        sums_kernel,
        in_specs=[hbm, hbm, vm],
        out_specs=[vm] * 5,
        out_shape=[
            jax.ShapeDtypeStruct((c + 8 + n // 2, c), jnp.float32),
            jax.ShapeDtypeStruct((n // 2, c), jnp.float32),
            jax.ShapeDtypeStruct((rows, c), jnp.float32),
            chunks,
            chunks,
        ],
        scratch_shapes=[
            pltpu.VMEM((rows * (n // COLS), COLS), jnp.float32),
            pltpu.VMEM((COLS // SUB, n // COLS, 8, COLS), jnp.float32),
            pltpu.VMEM((n, c), jnp.float32),
            pltpu.SemaphoreType.DMA((2, n // COLS)),
        ],
        compiler_params=pltpu.CompilerParams(vmem_limit_bytes=VMEM),
        name="sums",
    )(x, cot, mask)


def weight_kernel(gain_ref, w_ref, _, wt_ref):
    c = w_ref.shape[0]
    wg = w_ref[...].astype(jnp.float32) * jnp.broadcast_to(gain_ref[...], (c, c)).T
    wg = wg - jnp.mean(wg, axis=0, keepdims=True)
    high = wg.astype(jnp.bfloat16)
    wt_ref[:c] = high
    wt_ref[c:] = (wg - high.astype(jnp.float32)).astype(jnp.bfloat16)


def centred_weight(gain, w, dep):
    c = w.shape[0]
    vm = pl.BlockSpec(memory_space=pltpu.VMEM)
    return pl.pallas_call(
        weight_kernel,
        in_specs=[vm, vm, pl.BlockSpec(memory_space=pl.ANY)],
        out_specs=vm,
        out_shape=jax.ShapeDtypeStruct((2 * c, c), jnp.bfloat16),
        compiler_params=pltpu.CompilerParams(vmem_limit_bytes=SMALL),
        name="centred_weight",
    )(gain.reshape(1, c), w, dep)


def halve_kernel(payload_ref, got_ref, keep_ref, _, next_ref, kept_ref, *, parts):
    size = kept_ref.shape[0]
    next_ref[:parts] = payload_ref[:parts] + got_ref[:parts]
    next_ref[parts:] = keep_ref[size:] + got_ref[parts + size:]
    kept_ref[...] = keep_ref[:size] + got_ref[parts:parts + size]


def halve(payload, got, keep, dep, parts):
    size, c = keep.shape[0] // 2, keep.shape[1]
    vm = pl.BlockSpec(memory_space=pltpu.VMEM)
    return pl.pallas_call(
        functools.partial(halve_kernel, parts=parts),
        in_specs=[vm, vm, vm, pl.BlockSpec(memory_space=pl.ANY)],
        out_specs=[vm, vm],
        out_shape=[jax.ShapeDtypeStruct((parts + size, c), jnp.float32), jax.ShapeDtypeStruct((size, c), jnp.float32)],
        compiler_params=pltpu.CompilerParams(vmem_limit_bytes=SMALL),
        name="halve",
    )(payload, got, keep, dep)


def forward_kernel(payload_ref, got_ref, _, next_ref, row_ref, *, parts):
    rows = row_ref.shape[0]
    next_ref[:parts] = payload_ref[:parts] + got_ref[:parts]
    row_ref[...] = payload_ref[parts:parts + rows] + got_ref[parts:parts + rows]
    next_ref[parts:] = got_ref[parts + rows:]


def forward(payload, got, dep, parts, rows):
    size, c = payload.shape[0] - parts - rows, payload.shape[1]
    vm = pl.BlockSpec(memory_space=pltpu.VMEM)
    return pl.pallas_call(
        functools.partial(forward_kernel, parts=parts),
        in_specs=[vm, vm, pl.BlockSpec(memory_space=pl.ANY)],
        out_specs=[vm, vm],
        out_shape=[jax.ShapeDtypeStruct((parts + size, c), jnp.float32), jax.ShapeDtypeStruct((rows, c), jnp.float32)],
        compiler_params=pltpu.CompilerParams(vmem_limit_bytes=SMALL),
        name="forward",
    )(payload, got, dep)


def piece_kernel(*refs, first, count, before, last):
    refs = list(refs)
    xv, cv, mask_ref, wt_ref, _ = refs[:5]
    refs = refs[5:]
    prev = refs.pop(0) if before else None
    if before and first - before > 0:
        refs.pop(0)
    now = refs.pop(0)
    out = refs.pop(0) if before else None
    sems = refs.pop(0)
    rows, c = xv.shape[1], xv.shape[3]
    p = rows * COLS

    def away(buffer, t, j):
        return pltpu.make_async_copy(buffer.at[t], out.at[:, pl.ds(j * COLS, COLS)], sems.at[j])

    copies = [away(prev, t, first - before + t) for t in range(before)]
    for copy in copies:
        copy.start()
    for t in range(count):
        j = first + t
        both = lax.dot_general(wt_ref[...], cv[j].reshape(p, c), NT, preferred_element_type=jnp.float32)
        dc = both[:c] + both[c:]
        mask = jnp.concatenate(
            [mask_ref[i:i + 1, j * COLS:(j + 1) * COLS].astype(jnp.float32) for i in range(rows)], axis=1
        )
        xt = xv[j].reshape(p, c).T.astype(jnp.float32)
        xc = xt - jnp.sum(xt, axis=0, keepdims=True) * (1.0 / c)
        var = jnp.sum(xc * xc, axis=0, keepdims=True) * (1.0 / c)
        q = jnp.sum(xc * dc, axis=0, keepdims=True) * (1.0 / c)
        rstd = lax.rsqrt(var + EPS)
        masked = rstd * mask
        grad = (dc * masked - xc * (masked * rstd * rstd * q)).astype(jnp.bfloat16)
        now[t] = grad.T.reshape(rows, COLS, c)
        if last:
            copies.append(away(now, t, j))
            copies[-1].start()
    for copy in copies:
        copy.wait()


def piece(xv, cv, mask, wt, dep, prev, out, *, first, count):
    chunks, rows, cols, c = xv.shape
    n = chunks * cols
    vm = pl.BlockSpec(memory_space=pltpu.VMEM)
    hbm = pl.BlockSpec(memory_space=pl.ANY)
    before = 0 if prev is None else prev.shape[0]
    operands = [xv, cv, mask, wt, dep]
    in_specs = [vm] * 4 + [hbm]
    aliases = {}
    out_specs = [vm]
    out_shape = [jax.ShapeDtypeStruct((count, rows, cols, c), jnp.bfloat16)]
    if before:
        operands.append(prev)
        in_specs.append(vm)
        if out is not None:
            operands.append(out)
            in_specs.append(hbm)
            aliases = {6: 1}
        out_specs.append(hbm)
        out_shape.append(jax.ShapeDtypeStruct((rows, n, c), jnp.bfloat16))
    pairs = count * rows * cols
    results = pl.pallas_call(
        functools.partial(piece_kernel, first=first, count=count, before=before, last=first + count == chunks),
        in_specs=in_specs,
        out_specs=out_specs,
        out_shape=out_shape,
        scratch_shapes=[pltpu.SemaphoreType.DMA((chunks,))],
        input_output_aliases=aliases,
        compiler_params=pltpu.CompilerParams(vmem_limit_bytes=VMEM),
        cost_estimate=pl.CostEstimate(flops=6 * pairs * c * c, bytes_accessed=6 * pairs * c, transcendentals=0),
        name="gradient_piece",
    )(*operands)
    return results[0], (results[1] if before else None)


def tail_kernel(g_ref, got_ref, keep_ref, gain_ref, bias_ref, w_ref, right_ref, weight_ref, gains_ref, biases_ref, col_ref, *, scale):
    c = w_ref.shape[0]
    g = g_ref[:c] + got_ref[:c]
    total = g_ref[c:c + 1] + got_ref[c:c + 1]
    w = w_ref[...].astype(jnp.float32)
    gain = jnp.broadcast_to(gain_ref[...], (c, c)).T
    bias = jnp.broadcast_to(bias_ref[...], (c, c)).T
    weight_ref[...] = (gain * g + bias * total) * scale
    gains_ref[...] = jnp.sum((w * g).T, axis=0, keepdims=True) * scale
    biases_ref[...] = jnp.sum((w * total).T, axis=0, keepdims=True) * scale
    col_total = keep_ref[...] + got_ref[c + 8:]
    col_ref[...] = lax.dot_general(
        col_total, right_ref[...].astype(jnp.float32), NT,
        precision=lax.Precision.HIGHEST, preferred_element_type=jnp.float32,
    )


def tail(g, got, keep, gain, bias, w, right, scale):
    c = w.shape[0]
    vm = pl.BlockSpec(memory_space=pltpu.VMEM)
    weight, gains, biases, col = pl.pallas_call(
        functools.partial(tail_kernel, scale=scale),
        in_specs=[vm] * 7,
        out_specs=[vm] * 4,
        out_shape=[
            jax.ShapeDtypeStruct((c, c), jnp.float32),
            jax.ShapeDtypeStruct((1, c), jnp.float32),
            jax.ShapeDtypeStruct((1, c), jnp.float32),
            jax.ShapeDtypeStruct((keep.shape[0], right.shape[0]), jnp.float32),
        ],
        compiler_params=pltpu.CompilerParams(vmem_limit_bytes=SMALL),
        name="parameter_gradients",
    )(g, got, keep, gain.reshape(1, c), bias.reshape(1, c), w, right)
    return weight, gains.reshape(c), biases.reshape(c), col


def flipped(i, move):
    axis, bits = move
    x, z, y, core = i >> 5, ((i >> 4) & 1) * 2 + ((i >> 1) & 1), (i >> 2) & 3, i & 1
    x ^= bits if axis == "x" else 0
    y ^= bits if axis == "y" else 0
    z ^= bits if axis == "z" else 0
    core ^= bits if axis == "core" else 0
    return (((x * 2 + (z >> 1)) * 4 + y) * 2 + (z & 1)) * 2 + core


def exchange(value, move, other=None):
    moves = (move, other or move)
    pairs = [(i, flipped(i, moves[i & 1])) for i in range(128)]
    return lax.ppermute(value, ("row", "col"), pairs)


ORDER = (
    (("x", 1), ("y", 1)),
    (("y", 1), ("x", 1)),
    (("x", 3), ("y", 3)),
    (("y", 3), ("x", 3)),
)


PIECES = ((0, 2), (2, 2), (4, 1), (5, 1), (6, 1), (7, 1))


def shards(pair_act, pair_cot, pair_mask, gain, bias, w, left_weight, right_weight):
    rows, n, c = pair_act.shape
    pairs = rows * lax.axis_size("row") * n * lax.axis_size("col")
    scale = 1.0 / float(pairs) ** 0.5
    parts = c + 8
    payload, keep, row_part, xv, cv = sums(pair_act, pair_cot, pair_mask)
    wt = centred_weight(gain, w, payload)
    prev = out = None
    pieces = list(PIECES)

    def work(dep):
        first, count = pieces.pop(0)
        return piece(xv, cv, pair_mask, wt, dep, prev, out, first=first, count=count)

    for move, other in ORDER:
        got = exchange(payload, move, other)
        prev, out = work(payload)
        payload, keep = halve(payload, got, keep, prev, parts)
    send = payload[parts:]
    payload = jnp.concatenate([payload[:parts], row_part], axis=0)
    payload = payload + exchange(payload, ("core", 1))
    payload = jnp.concatenate([payload, send], axis=0)
    got = exchange(payload, ("z", 1))
    prev, out = work(payload)
    payload, row_total = forward(payload, got, prev, parts, rows)
    got = exchange(payload, ("z", 3))
    prev, out = work(payload)

    row_single_grad = jnp.einsum(
        "rc,sc->rs", row_total, left_weight.astype(jnp.float32), precision=lax.Precision.HIGHEST
    )
    weight_grad, gain_grad, bias_grad, col_single_grad = tail(payload, got, keep, gain, bias, w, right_weight, scale)
    return out, row_single_grad, col_single_grad, weight_grad, gain_grad, bias_grad


def solution(mesh):
    in_specs = (
        P("row", "col", None),
        P("row", "col", None),
        P("row", "col"),
        P(),
        P(),
        P(),
        P(),
        P(),
    )
    out_specs = (P("row", "col", None), P("row", None), P(("col", "row"), None), P(), P(), P())
    return jax.shard_map(shards, mesh=mesh, in_specs=in_specs, out_specs=out_specs, check_vma=False)
```

time: 60.7 us -> 50.8 us (0.84)
  starting transfers between devices: 23.5 us -> 15.6 us
  other arithmetic: 2.63 us -> 0.03 us
  waiting for transfers between devices: 8.88 us -> 11.3 us
  Pallas kernels: 23.1 us -> 21.1 us
  local copies, waits for them, and re-layouts: 0.02 us -> 0.95 us
  matrix products: 1.68 us -> 0.84 us
    ppermute x12 -> x7, starting transfers between devices: 23.5 us -> 15.6 us  [exchange(): return lax.ppermute(value, ('row', 'col'), pairs)]
    add x11 -> x1, other arithmetic: 2.63 us -> 0.01 us  [shards(): payload = payload + exchange(payload, ('core', 1))]
    ppermute x12 -> x7, waiting for transfers between devices: 8.88 us -> 11.3 us  [exchange(): return lax.ppermute(value, ('row', 'col'), pairs)]
    pallas_call x2 -> x13, Pallas kernels: 21.5 us -> 20.1 us  [the longest x6 11.5 us: piece(): pl.pallas_call(functools.partial(piece_kernel, first=first, count=count,...]
    unnamed x4 -> x12, local copies, waits for them, and re-layouts: 0.01 us -> 0.94 us
    dot_general x1 -> x0, matrix products: 0.84 us -> none  [shards(): jnp.einsum('rc,sc->rs', col_total, right_weight.astype(jnp.float32), prec...]
    pallas_call x1, Pallas kernels: 1.64 us -> 0.95 us  [tail(): pl.pallas_call(functools.partial(tail_kernel, scale=scale), in_specs=[vm]...]
  transfers between devices with their start and end apart: 12 -> 7, of which waited for: 7 -> 6; matrix products, arithmetic and copies ran while one was open for 6% -> 2% of each run, Pallas kernels for 19% -> 23%
where the time goes in v2:
time: 50.8 us; the launch traced here: 50.6 us
  Pallas kernels  21.1 us (42%)
  starting transfers between devices  15.6 us (31%)
  waiting for transfers between devices  11.3 us (22%)
  local copies, waits for them, and re-layouts  0.95 us (2%)
  matrix products  0.84 us (2%)
  between operations  0.8 us (2%)
    ppermute x7, starting transfers between devices, exchange(): return lax.ppermute(value, ('row', 'col'), pairs)  15.6 us
    pallas_call x6, Pallas kernels, piece(): pl.pallas_call(functools.partial(piece_kernel, first=first, count=count,...  11.5 us
    ppermute x7, waiting for transfers between devices, exchange(): return lax.ppermute(value, ('row', 'col'), pairs)  11.3 us
    pallas_call x1, Pallas kernels, sums(): pl.pallas_call(sums_kernel, in_specs=[hbm, hbm, vm], out_specs=[vm] * 5,...  8.45 us
  transfers between devices with their start and end apart: 7, of which 6 were waited for; matrix products, arithmetic and copies ran while one was open for 2% of the time, Pallas kernels for 23%

profile of v2, /device:TPU:0, one launch (start us, length us, event | category | flops | bytes accessed | tf_op | source)
XLA Modules:
  0.0 50.6 jit_solution(11976816927263166271)
XLA Ops:
  0.6 0.0 copy-start
  0.6 0.0 copy-start.1
  0.7 0.9 %copy-done.1 = s32[24,1024]{1,0:T(8,128)S(1)} copy-done((s32[24,1024]{1,0:T(8,128)S(1)}, s32[24,1024]{1,0:T(8,128)}, u32[]{:S(2)}) %copy-start.1) | copy-done | bytes 98328
  1.6 8.5 %sums.1 = (f32[648,128]{1,0:T(8,128)S(1)}, f32[512,128]{1,0:T(8,128)S(1)}, f32[24,128]{1,0:T(8,128)S(1)}, bf16[8,24,128,128]{3,2,1,0:T(8,128)(2,1)S(1)}, bf16[8,24,128,128]{3,2,1,0:T(8,128)(2,1)S(1)}) custom-call(bf16[24,1024,128]{2,1,0:T(8,128)(2,1)} %x_hbm.1, bf16[24,1024,128]{2,1,0:T(8,128)(2,1)} %cot_hbm.1, s32[24,1024]{1,0:T(8,128)S(1)} %copy-done.1), custom_call_target="tpu_custom_call" | custom-call | tf_op jit(solution)/shard_map/sums/pallas_call | solution.py:102
  10.0 1.7 %collective-permute-start = (f32[648,128]{1,0:T(8,128)S(1)}, f32[648,128]{1,0:T(8,128)S(1)}, u32[]{:S(2)}, u32[]{:S(2)}) collective-permute-start(f32[648,128]{1,0:T(8,128)S(1)} %get-tuple-element.36._.refs_4_.payload_ref), channel_id=1, source_target_pairs={{0,32},{1,5},{2,34},{3,7},{4,36},{5,1},{6,38},{7,3},{8,40},{9,13},... | collective-permute-start | bytes 995336 | tf_op jit(solution)/shard_map/ppermute | solution.py:311
  11.7 0.0 copy-done.2
  11.7 0.0 copy-done.4
  11.7 0.1 centred_weight.1.refs_3_
  11.8 2.0 %gradient_piece.6._.refs_5_ = bf16[2,24,128,128]{3,2,1,0:T(8,128)(2,1)S(1)} custom-call(bf16[8,24,128,128]{3,2,1,0:T(8,128)(2,1)S(1)} %get-tuple-element.34.refs_0_, bf16[8,24,128,128]{3,2,1,0:T(8,128)(2,1)S(1)} %get-tuple-element.35.refs_1_, s32[24,1024]{1,0:T(8,128)S(1)} %copy-done.1, bf16[256,128]{1,0:T(8,128)(2,1)S(1)} %centred_weight.1.refs_3_, ...), custom_call_target="tpu_custom_call" | custom-call | flops 603979776 | bytes 4718592 | tf_op jit(solution)/shard_map/gradient_piece/pallas_call | solution.py:248
  13.8 3.4 %collective-permute-done.got_ref = f32[648,128]{1,0:T(8,128)S(1)} collective-permute-done((f32[648,128]{1,0:T(8,128)S(1)}, f32[648,128]{1,0:T(8,128)S(1)}, u32[]{:S(2)}, u32[]{:S(2)}) %collective-permute-start) | collective-permute-done | bytes 331808 | tf_op jit(solution)/shard_map/ppermute | solution.py:311
  17.3 1.7 %collective-permute-start.1 = (f32[392,128]{1,0:T(8,128)S(1)}, f32[392,128]{1,0:T(8,128)S(1)}, u32[]{:S(2)}, u32[]{:S(2)}) collective-permute-start(f32[392,128]{1,0:T(8,128)S(1)} %get-tuple-element.38.refs_4_.payload_ref), channel_id=1, source_target_pairs={{0,4},{1,33},{2,6},{3,35},{4,0},{5,37},{6,2},{7,39},{8,12},{9,41},... | collective-permute-start | bytes 602120 | tf_op jit(solution)/shard_map/ppermute | solution.py:311
  19.0 2.6 %gradient_piece.7 = (bf16[2,24,128,128]{3,2,1,0:T(8,128)(2,1)S(1)}, bf16[24,1024,128]{2,1,0:T(8,128)(2,1)}) custom-call(bf16[8,24,128,128]{3,2,1,0:T(8,128)(2,1)S(1)} %get-tuple-element.34.refs_0_, bf16[8,24,128,128]{3,2,1,0:T(8,128)(2,1)S(1)} %get-tuple-element.35.refs_1_, s32[24,1024]{1,0:T(8,128)S(1)} %copy-done.1, ...), custom_call_target="tpu_custom_call" | custom-call | flops 603979776 | bytes 4718592 | tf_op jit(solution)/shard_map/gradient_piece/pallas_call | solution.py:248
  21.6 1.5 %collective-permute-done.1.got_ref = f32[392,128]{1,0:T(8,128)S(1)} collective-permute-done((f32[392,128]{1,0:T(8,128)S(1)}, f32[392,128]{1,0:T(8,128)S(1)}, u32[]{:S(2)}, u32[]{:S(2)}) %collective-permute-start.1) | collective-permute-done | bytes 200736 | tf_op jit(solution)/shard_map/ppermute | solution.py:311
  23.1 2.9 %collective-permute-start.2 = (f32[264,128]{1,0:T(8,128)S(1)}, f32[264,128]{1,0:T(8,128)S(1)}, u32[]{:S(2)}, u32[]{:S(2)}) collective-permute-start(f32[264,128]{1,0:T(8,128)S(1)} %get-tuple-element.41.refs_4_.payload_ref), channel_id=1, source_target_pairs={{0,96},{1,13},{2,98},{3,15},{4,100},{5,9},{6,102},{7,11},{8,104},{... | collective-permute-start | bytes 405512 | tf_op jit(solution)/shard_map/ppermute | solution.py:311
  26.0 1.5 %gradient_piece.8 = (bf16[1,24,128,128]{3,2,1,0:T(8,128)(2,1)S(1)}, bf16[24,1024,128]{2,1,0:T(8,128)(2,1)}) custom-call(bf16[8,24,128,128]{3,2,1,0:T(8,128)(2,1)S(1)} %get-tuple-element.34.refs_0_, bf16[8,24,128,128]{3,2,1,0:T(8,128)(2,1)S(1)} %get-tuple-element.35.refs_1_, s32[24,1024]{1,0:T(8,128)S(1)} %copy-done.1, ...), custom_call_target="tpu_custom_call", output_to_operand_aliasing={{1}: (6, {})} | custom-call | flops 301989888 | bytes 2359296 | tf_op jit(solution)/shard_map/gradient_piece/pallas_call | solution.py:248
  27.5 1.9 %collective-permute-done.2.got_ref = f32[264,128]{1,0:T(8,128)S(1)} collective-permute-done((f32[264,128]{1,0:T(8,128)S(1)}, f32[264,128]{1,0:T(8,128)S(1)}, u32[]{:S(2)}, u32[]{:S(2)}) %collective-permute-start.2) | collective-permute-done | bytes 135200 | tf_op jit(solution)/shard_map/ppermute | solution.py:311
  29.4 3.2 %collective-permute-start.3 = (f32[200,128]{1,0:T(8,128)S(1)}, f32[200,128]{1,0:T(8,128)S(1)}, u32[]{:S(2)}, u32[]{:S(2)}) collective-permute-start(f32[200,128]{1,0:T(8,128)S(1)} %get-tuple-element.45.refs_4_.payload_ref), channel_id=1, source_target_pairs={{0,12},{1,97},{2,14},{3,99},{4,8},{5,101},{6,10},{7,103},{8,4},{9,... | collective-permute-start | bytes 307208 | tf_op jit(solution)/shard_map/ppermute | solution.py:311
  32.6 1.2 %gradient_piece.9 = (bf16[1,24,128,128]{3,2,1,0:T(8,128)(2,1)S(1)}, bf16[24,1024,128]{2,1,0:T(8,128)(2,1)}) custom-call(bf16[8,24,128,128]{3,2,1,0:T(8,128)(2,1)S(1)} %get-tuple-element.34.refs_0_, bf16[8,24,128,128]{3,2,1,0:T(8,128)(2,1)S(1)} %get-tuple-element.35.refs_1_, s32[24,1024]{1,0:T(8,128)S(1)} %copy-done.1, ...), custom_call_target="tpu_custom_call", output_to_operand_aliasing={{1}: (6, {})} | custom-call | flops 301989888 | bytes 2359296 | tf_op jit(solution)/shard_map/gradient_piece/pallas_call | solution.py:248
  33.9 1.5 %collective-permute-done.3.got_ref = f32[200,128]{1,0:T(8,128)S(1)} collective-permute-done((f32[200,128]{1,0:T(8,128)S(1)}, f32[200,128]{1,0:T(8,128)S(1)}, u32[]{:S(2)}, u32[]{:S(2)}) %collective-permute-start.3) | collective-permute-done | bytes 102432 | tf_op jit(solution)/shard_map/ppermute | solution.py:311
  35.4 0.1 collective-permute-start.4
  35.5 1.3 %collective-permute-done.4 = f32[160,128]{1,0:T(8,128)S(1)} collective-permute-done((f32[160,128]{1,0:T(8,128)S(1)}, f32[160,128]{1,0:T(8,128)S(1)}, u32[]{:S(2)}, u32[]{:S(2)}) %collective-permute-start.4) | collective-permute-done | bytes 81952 | tf_op jit(solution)/shard_map/ppermute | solution.py:311
  36.8 2.1 %collective-permute-start.5 = (f32[192,128]{1,0:T(8,128)S(1)}, f32[192,128]{1,0:T(8,128)S(1)}, u32[]{:S(2)}, u32[]{:S(2)}) collective-permute-start(f32[192,128]{1,0:T(8,128)S(1)} %pad_maximum_fusion.refs_4_.payload_ref), channel_id=1, source_target_pairs={{0,2},{1,3},{2,0},{3,1},{4,6},{5,7},{6,4},{7,5},{8,10},{9,11},{10,... | collective-permute-start | bytes 294920 | tf_op jit(solution)/shard_map/ppermute | solution.py:311
  38.9 1.2 %gradient_piece.10 = (bf16[1,24,128,128]{3,2,1,0:T(8,128)(2,1)S(1)}, bf16[24,1024,128]{2,1,0:T(8,128)(2,1)}) custom-call(bf16[8,24,128,128]{3,2,1,0:T(8,128)(2,1)S(1)} %get-tuple-element.34.refs_0_, bf16[8,24,128,128]{3,2,1,0:T(8,128)(2,1)S(1)} %get-tuple-element.35.refs_1_, s32[24,1024]{1,0:T(8,128)S(1)} %copy-done.1, ...), custom_call_target="tpu_custom_call", output_to_operand_aliasing={{1}: (6, {})} | custom-call | flops 301989888 | bytes 2359296 | tf_op jit(solution)/shard_map/gradient_piece/pallas_call | solution.py:248
  40.1 1.9 %collective-permute-done.5.got_ref = f32[192,128]{1,0:T(8,128)S(1)} collective-permute-done((f32[192,128]{1,0:T(8,128)S(1)}, f32[192,128]{1,0:T(8,128)S(1)}, u32[]{:S(2)}, u32[]{:S(2)}) %collective-permute-start.5) | collective-permute-done | bytes 98336 | tf_op jit(solution)/shard_map/ppermute | solution.py:311
  42.0 3.9 %collective-permute-start.6 = (f32[168,128]{1,0:T(8,128)S(1)}, f32[168,128]{1,0:T(8,128)S(1)}, u32[]{:S(2)}, u32[]{:S(2)}) collective-permute-start(f32[168,128]{1,0:T(8,128)S(1)} %get-tuple-element.53.refs_4_.g_ref), channel_id=1, source_target_pairs={{0,18},{1,19},{2,16},{3,17},{4,22},{5,23},{6,20},{7,21},{8,26},{9,... | collective-permute-start | bytes 258056 | tf_op jit(solution)/shard_map/ppermute | solution.py:311
  46.0 0.0 copy-done
  46.0 0.8 %fusion.1 = f32[24,384]{1,0:T(8,128)} fusion(f32[24,128]{1,0:T(8,128)S(1)} %get-tuple-element.56, bf16[384,128]{1,0:T(8,128)(2,1)S(1)} %copy-done), kind=kOutput, calls=%fused_computation.3 | convolution fusion | flops 14155776 | bytes 147456 | tf_op jit(solution)/shard_map/rc,sc->rs/dot_general | solution.py:353
  46.8 2.8 %gradient_piece.11 = (bf16[1,24,128,128]{3,2,1,0:T(8,128)(2,1)}, bf16[24,1024,128]{2,1,0:T(8,128)(2,1)}) custom-call(bf16[8,24,128,128]{3,2,1,0:T(8,128)(2,1)S(1)} %get-tuple-element.34.refs_0_, bf16[8,24,128,128]{3,2,1,0:T(8,128)(2,1)S(1)} %get-tuple-element.35.refs_1_, s32[24,1024]{1,0:T(8,128)S(1)} %copy-done.1, ...), custom_call_target="tpu_custom_call", output_to_operand_aliasing={{1}: (6, {})} | custom-call | flops 301989888 | bytes 2359296 | tf_op jit(solution)/shard_map/gradient_piece/pallas_call | solution.py:248
  49.7 0.0 collective-permute-done.6.got_ref
  49.7 0.0 copy-done.3
  49.7 0.0 copy-done.5
  49.7 1.0 %parameter_gradients.1 = (f32[128,128]{1,0:T(8,128)}, f32[1,128]{1,0:T(1,128)}, f32[1,128]{1,0:T(1,128)}, f32[32,384]{1,0:T(8,128)}) custom-call(f32[168,128]{1,0:T(8,128)S(1)} %get-tuple-element.53.refs_4_.g_ref, f32[168,128]{1,0:T(8,128)S(1)} %collective-permute-done.6.got_ref, f32[32,128]{1,0:T(8,128)S(1)} %get-tuple-element.57.keep_ref, ...), custom_call_target="tpu_custom_call" | custom-call | tf_op jit(solution)/shard_map/parameter_gradients/pallas_call | solution.py:282
  (14 shorter events, 0.2 us)
Async XLA Ops:
  0.6 45.3 %copy-start = (bf16[384,128]{1,0:T(8,128)(2,1)S(1)}, bf16[384,128]{1,0:T(8,128)(2,1)}, u32[]{:S(2)}) copy-start(bf16[384,128]{1,0:T(8,128)(2,1)} %param.14) | copy-start | bytes 294916
  0.6 0.9 %copy-start.1 = (s32[24,1024]{1,0:T(8,128)S(1)}, s32[24,1024]{1,0:T(8,128)}, u32[]{:S(2)}) copy-start(s32[24,1024]{1,0:T(8,128)} %refs_2_.11) | copy-start | bytes 294916
  1.6 10.1 %copy-start.2 = (bf16[128,128]{1,0:T(8,128)(2,1)S(1)}, bf16[128,128]{1,0:T(8,128)(2,1)}, u32[]{:S(2)}) copy-start(bf16[128,128]{1,0:T(8,128)(2,1)} %w_ref.3) | copy-start | bytes 98308
  1.6 10.1 %copy-start.4 = (f32[128]{0:T(128)S(1)}, f32[128]{0:T(128)}, u32[]{:S(2)}) copy-start(f32[128]{0:T(128)} %param.11) | copy-start | bytes 1540
  10.0 7.2 %collective-permute-start = (f32[648,128]{1,0:T(8,128)S(1)}, f32[648,128]{1,0:T(8,128)S(1)}, u32[]{:S(2)}, u32[]{:S(2)}) collective-permute-start(f32[648,128]{1,0:T(8,128)S(1)} %get-tuple-element.36._.refs_4_.payload_ref), channel_id=1, source_target_pairs={{0,32},{1,5},{2,34},{3,7},{4,36},{5,1},{6,38},{7,3},{8,40},{9,13},... | collective-permute-start | bytes 995336 | tf_op jit(solution)/shard_map/ppermute | solution.py:311
  17.3 5.8 %collective-permute-start.1 = (f32[392,128]{1,0:T(8,128)S(1)}, f32[392,128]{1,0:T(8,128)S(1)}, u32[]{:S(2)}, u32[]{:S(2)}) collective-permute-start(f32[392,128]{1,0:T(8,128)S(1)} %get-tuple-element.38.refs_4_.payload_ref), channel_id=1, source_target_pairs={{0,4},{1,33},{2,6},{3,35},{4,0},{5,37},{6,2},{7,39},{8,12},{9,41},... | collective-permute-start | bytes 602120 | tf_op jit(solution)/shard_map/ppermute | solution.py:311
  23.1 6.3 %collective-permute-start.2 = (f32[264,128]{1,0:T(8,128)S(1)}, f32[264,128]{1,0:T(8,128)S(1)}, u32[]{:S(2)}, u32[]{:S(2)}) collective-permute-start(f32[264,128]{1,0:T(8,128)S(1)} %get-tuple-element.41.refs_4_.payload_ref), channel_id=1, source_target_pairs={{0,96},{1,13},{2,98},{3,15},{4,100},{5,9},{6,102},{7,11},{8,104},{... | collective-permute-start | bytes 405512 | tf_op jit(solution)/shard_map/ppermute | solution.py:311
  29.4 6.0 %collective-permute-start.3 = (f32[200,128]{1,0:T(8,128)S(1)}, f32[200,128]{1,0:T(8,128)S(1)}, u32[]{:S(2)}, u32[]{:S(2)}) collective-permute-start(f32[200,128]{1,0:T(8,128)S(1)} %get-tuple-element.45.refs_4_.payload_ref), channel_id=1, source_target_pairs={{0,12},{1,97},{2,14},{3,99},{4,8},{5,101},{6,10},{7,103},{8,4},{9,... | collective-permute-start | bytes 307208 | tf_op jit(solution)/shard_map/ppermute | solution.py:311
  35.4 1.4 %collective-permute-start.4 = (f32[160,128]{1,0:T(8,128)S(1)}, f32[160,128]{1,0:T(8,128)S(1)}, u32[]{:S(2)}, u32[]{:S(2)}) collective-permute-start(f32[160,128]{1,0:T(8,128)S(1)} %pad_maximum_fusion.1), channel_id=1, source_target_pairs={{0,1},{1,0},{2,3},{3,2},{4,5},{5,4},{6,7},{7,6},{8,9},{9,8},{10,11... | collective-permute-start | bytes 245768 | tf_op jit(solution)/shard_map/ppermute | solution.py:311
  36.8 5.2 %collective-permute-start.5 = (f32[192,128]{1,0:T(8,128)S(1)}, f32[192,128]{1,0:T(8,128)S(1)}, u32[]{:S(2)}, u32[]{:S(2)}) collective-permute-start(f32[192,128]{1,0:T(8,128)S(1)} %pad_maximum_fusion.refs_4_.payload_ref), channel_id=1, source_target_pairs={{0,2},{1,3},{2,0},{3,1},{4,6},{5,7},{6,4},{7,5},{8,10},{9,11},{10,... | collective-permute-start | bytes 294920 | tf_op jit(solution)/shard_map/ppermute | solution.py:311
  42.0 7.6 %collective-permute-start.6 = (f32[168,128]{1,0:T(8,128)S(1)}, f32[168,128]{1,0:T(8,128)S(1)}, u32[]{:S(2)}, u32[]{:S(2)}) collective-permute-start(f32[168,128]{1,0:T(8,128)S(1)} %get-tuple-element.53.refs_4_.g_ref), channel_id=1, source_target_pairs={{0,18},{1,19},{2,16},{3,17},{4,22},{5,23},{6,20},{7,21},{8,26},{9,... | collective-permute-start | bytes 258056 | tf_op jit(solution)/shard_map/ppermute | solution.py:311
  46.8 2.9 %copy-start.3 = (bf16[384,128]{1,0:T(8,128)(2,1)S(1)}, bf16[384,128]{1,0:T(8,128)(2,1)}, u32[]{:S(2)}) copy-start(bf16[384,128]{1,0:T(8,128)(2,1)} %right_ref.1) | copy-start | bytes 294916
  46.8 2.9 %copy-start.5 = (f32[128]{0:T(128)S(1)}, f32[128]{0:T(128)}, u32[]{:S(2)}) copy-start(f32[128]{0:T(128)} %param.12) | copy-start | bytes 1540

commit v3 on v2

--- a/solution.py
+++ b/solution.py
@@ -11,12 +11,13 @@
 NT = (((1,), (1,)), ((), ()))
 COLS = 128
 SUB = 32
-VMEM = 38 << 20
+HOLD = 38 << 20
+PIECE = 16 << 20
 SMALL = 4 << 20
 
 
 def sums_kernel(
-    x_hbm, cot_hbm, mask_ref, first_ref, keep_ref, row_ref, xv, cv, mf, mv, cc, sems
+    x_hbm, cot_hbm, mask_hbm, g_ref, send_ref, keep_ref, xv, cv, mask_ref, mf, mv, cc, sems, mask_sem
 ):
     rows, n, c = x_hbm.shape
     chunks = n // COLS
@@ -31,9 +32,12 @@
             pltpu.make_async_copy(cot_hbm.at[:, cols], cv.at[j], sems.at[1, j]),
         )
 
+    mask_copy = pltpu.make_async_copy(mask_hbm, mask_ref, mask_sem)
+    mask_copy.start()
     for j in range(chunks):
         for copy in copies(j):
             copy.start()
+    mask_copy.wait()
     lane = lax.broadcasted_iota(jnp.int32, (bands, COLS), 1) // SUB
     for j in range(chunks):
         mf[j * rows:(j + 1) * rows, :] = mask_ref[:, j * COLS:(j + 1) * COLS].astype(jnp.float32)
@@ -45,8 +49,7 @@
                 moved = strips[i] if shift == 0 else pltpu.roll(strips[i], shift, 1)
                 mixed = jnp.where(lane == i, moved, mixed)
             mv[q, j, :bands, :] = mixed
-    first_ref[:c + 8] = jnp.zeros((c + 8, c), jnp.float32)
-    row_ref[...] = jnp.zeros_like(row_ref)
+    g_ref[...] = jnp.zeros_like(g_ref)
     wide_lane = lax.broadcasted_iota(jnp.int32, (SUB, k), 1)
     wide_sub = lax.broadcasted_iota(jnp.int32, (SUB, k), 0)
     pattern = jnp.concatenate(
@@ -86,12 +89,12 @@
             s1 = jnp.where(core == 0, y1, x1)
             off = pl.multiple_of((s4 * 16 + s3 * 8 + s2 * 4 + s1 * 2 + z) * SUB, SUB)
             cc[pl.ds(off, SUB), :] = columns[q]
-        first_ref[:c] += total[:c]
-        row_ref[...] += total[c:c + rows]
+        g_ref[:c] += total[:c]
+        g_ref[c + 8:] += total[c:c + rows]
 
     keep_ref[...] = cc[:n // 2]
-    first_ref[c + 8:] = cc[n // 2:]
-    first_ref[c:c + 8] = jnp.broadcast_to(jnp.sum(row_ref[...], axis=0, keepdims=True), (8, c))
+    send_ref[...] = cc[n // 2:]
+    g_ref[c:c + 8] = jnp.broadcast_to(jnp.sum(g_ref[c + 8:], axis=0, keepdims=True), (8, c))
 
 
 def sums(x, cot, mask):
@@ -101,22 +104,24 @@
     chunks = jax.ShapeDtypeStruct((n // COLS, rows, COLS, c), jnp.bfloat16)
     return pl.pallas_call(
         sums_kernel,
-        in_specs=[hbm, hbm, vm],
+        in_specs=[hbm, hbm, hbm],
         out_specs=[vm] * 5,
         out_shape=[
-            jax.ShapeDtypeStruct((c + 8 + n // 2, c), jnp.float32),
+            jax.ShapeDtypeStruct((c + 8 + rows, c), jnp.float32),
             jax.ShapeDtypeStruct((n // 2, c), jnp.float32),
-            jax.ShapeDtypeStruct((rows, c), jnp.float32),
+            jax.ShapeDtypeStruct((n // 2, c), jnp.float32),
             chunks,
             chunks,
         ],
         scratch_shapes=[
+            pltpu.VMEM((rows, n), jnp.int32),
             pltpu.VMEM((rows * (n // COLS), COLS), jnp.float32),
             pltpu.VMEM((COLS // SUB, n // COLS, 8, COLS), jnp.float32),
             pltpu.VMEM((n, c), jnp.float32),
             pltpu.SemaphoreType.DMA((2, n // COLS)),
+            pltpu.SemaphoreType.DMA,
         ],
-        compiler_params=pltpu.CompilerParams(vmem_limit_bytes=VMEM),
+        compiler_params=pltpu.CompilerParams(vmem_limit_bytes=HOLD),
         name="sums",
     )(x, cot, mask)
 
@@ -143,24 +148,25 @@
     )(gain.reshape(1, c), w, dep)
 
 
-def halve_kernel(payload_ref, got_ref, keep_ref, _, next_ref, kept_ref, *, parts):
+def halve_kernel(payload_ref, got_ref, col_ref, keep_ref, _, next_ref, kept_ref, *, parts):
     size = kept_ref.shape[0]
+    at = col_ref.shape[0] - 2 * size
     next_ref[:parts] = payload_ref[:parts] + got_ref[:parts]
-    next_ref[parts:] = keep_ref[size:] + got_ref[parts + size:]
-    kept_ref[...] = keep_ref[:size] + got_ref[parts:parts + size]
-
-
-def halve(payload, got, keep, dep, parts):
+    next_ref[parts:] = keep_ref[size:] + col_ref[at + size:]
+    kept_ref[...] = keep_ref[:size] + col_ref[at:at + size]
+
+
+def halve(payload, got, col, keep, dep, parts):
     size, c = keep.shape[0] // 2, keep.shape[1]
     vm = pl.BlockSpec(memory_space=pltpu.VMEM)
     return pl.pallas_call(
         functools.partial(halve_kernel, parts=parts),
-        in_specs=[vm, vm, vm, pl.BlockSpec(memory_space=pl.ANY)],
+        in_specs=[vm, vm, vm, vm, pl.BlockSpec(memory_space=pl.ANY)],
         out_specs=[vm, vm],
         out_shape=[jax.ShapeDtypeStruct((parts + size, c), jnp.float32), jax.ShapeDtypeStruct((size, c), jnp.float32)],
         compiler_params=pltpu.CompilerParams(vmem_limit_bytes=SMALL),
         name="halve",
-    )(payload, got, keep, dep)
+    )(payload, got, col, keep, dep)
 
 
 def forward_kernel(payload_ref, got_ref, _, next_ref, row_ref, *, parts):
@@ -252,7 +258,7 @@
         out_shape=out_shape,
         scratch_shapes=[pltpu.SemaphoreType.DMA((chunks,))],
         input_output_aliases=aliases,
-        compiler_params=pltpu.CompilerParams(vmem_limit_bytes=VMEM),
+        compiler_params=pltpu.CompilerParams(vmem_limit_bytes=PIECE),
         cost_estimate=pl.CostEstimate(flops=6 * pairs * c * c, bytes_accessed=6 * pairs * c, transcendentals=0),
         name="gradient_piece",
     )(*operands)
@@ -319,7 +325,7 @@
 )
 
 
-PIECES = ((0, 2), (2, 2), (4, 1), (5, 1), (6, 1), (7, 1))
+PIECES = ((0, 3), (3, 2), (5, 2), (7, 1))
 
 
 def shards(pair_act, pair_cot, pair_mask, gain, bias, w, left_weight, right_weight):
@@ -327,28 +333,21 @@
     pairs = rows * lax.axis_size("row") * n * lax.axis_size("col")
     scale = 1.0 / float(pairs) ** 0.5
     parts = c + 8
-    payload, keep, row_part, xv, cv = sums(pair_act, pair_cot, pair_mask)
-    wt = centred_weight(gain, w, payload)
+    sums_here, send, keep, xv, cv = sums(pair_act, pair_cot, pair_mask)
+    wt = centred_weight(gain, w, sums_here)
     prev = out = None
-    pieces = list(PIECES)
-
-    def work(dep):
-        first, count = pieces.pop(0)
-        return piece(xv, cv, pair_mask, wt, dep, prev, out, first=first, count=count)
-
-    for move, other in ORDER:
+    col = exchange(send, *ORDER[0])
+    sums_here = sums_here + exchange(sums_here, ("core", 1))
+    payload, row_part = sums_here[:parts], sums_here[parts:]
+    for step, (move, other) in enumerate(ORDER):
         got = exchange(payload, move, other)
-        prev, out = work(payload)
-        payload, keep = halve(payload, got, keep, prev, parts)
-    send = payload[parts:]
-    payload = jnp.concatenate([payload[:parts], row_part], axis=0)
-    payload = payload + exchange(payload, ("core", 1))
-    payload = jnp.concatenate([payload, send], axis=0)
+        first, count = PIECES[step]
+        prev, out = piece(xv, cv, pair_mask, wt, payload, prev, out, first=first, count=count)
+        payload, keep = halve(payload, got, got if step else col, keep, prev, parts)
+    payload = jnp.concatenate([payload[:parts], row_part, payload[parts:]], axis=0)
     got = exchange(payload, ("z", 1))
-    prev, out = work(payload)
     payload, row_total = forward(payload, got, prev, parts, rows)
     got = exchange(payload, ("z", 3))
-    prev, out = work(payload)
 
     row_single_grad = jnp.einsum(
         "rc,sc->rs", row_total, left_weight.astype(jnp.float32), precision=lax.Precision.HIGHEST

time: 50.8 us -> 48 us (0.945)
  Pallas kernels: 21.1 us -> 19.2 us
  waiting for transfers between devices: 11.3 us -> 10 us
    pallas_call x6 -> x4, Pallas kernels: 11.5 us -> 9.49 us  [piece(): pl.pallas_call(functools.partial(piece_kernel, first=first, count=count,...]
    ppermute x7 -> x8, waiting for transfers between devices: 11.3 us -> 10 us  [exchange(): return lax.ppermute(value, ('row', 'col'), pairs)]
    ppermute x7 -> x8, starting transfers between devices: 15.6 us -> 16.1 us  [exchange(): return lax.ppermute(value, ('row', 'col'), pairs)]
  transfers between devices with their start and end apart: 7 -> 8, of which waited for: 6 -> 7; matrix products, arithmetic and copies ran while one was open for 2% -> 2% of each run, Pallas kernels for 23% -> 20%
where the time goes in v3:
time: 48 us; the launch traced here: 47.9 us
  Pallas kernels  19.2 us (40%)
  starting transfers between devices  16.1 us (34%)
  waiting for transfers between devices  10 us (21%)
  local copies, waits for them, and re-layouts  0.97 us (2%)
  matrix products  0.84 us (2%)
  between operations  0.77 us (2%)
    ppermute x8, starting transfers between devices, exchange(): return lax.ppermute(value, ('row', 'col'), pairs)  16.1 us
    ppermute x8, waiting for transfers between devices, exchange(): return lax.ppermute(value, ('row', 'col'), pairs)  10 us
    pallas_call x4, Pallas kernels, piece(): pl.pallas_call(functools.partial(piece_kernel, first=first, count=count,...  9.49 us
    pallas_call x1, Pallas kernels, sums(): pl.pallas_call(sums_kernel, in_specs=[hbm, hbm, hbm], out_specs=[vm] * 5,...  8.49 us
  transfers between devices with their start and end apart: 8, of which 7 were waited for; matrix products, arithmetic and copies ran while one was open for 2% of the time, Pallas kernels for 20%

profile of v3, /device:TPU:0, one launch (start us, length us, event | category | flops | bytes accessed | tf_op | source)
XLA Modules:
  0.0 47.9 jit_solution(6860046348490802427)
XLA Ops:
  0.6 0.0 copy-start
  0.6 0.0 copy-start.1
  0.7 0.9 %copy-done.1 = s32[24,1024]{1,0:T(8,128)S(1)} copy-done((s32[24,1024]{1,0:T(8,128)S(1)}, s32[24,1024]{1,0:T(8,128)}, u32[]{:S(2)}) %copy-start.1) | copy-done | bytes 98328
  1.6 8.5 %sums.1 = (f32[160,128]{1,0:T(8,128)S(1)}, f32[512,128]{1,0:T(8,128)S(1)}, f32[512,128]{1,0:T(8,128)S(1)}, bf16[8,24,128,128]{3,2,1,0:T(8,128)(2,1)S(1)}, bf16[8,24,128,128]{3,2,1,0:T(8,128)(2,1)S(1)}) custom-call(bf16[24,1024,128]{2,1,0:T(8,128)(2,1)} %x_hbm.1, bf16[24,1024,128]{2,1,0:T(8,128)(2,1)} %cot_hbm.1, s32[24,1024]{1,0:T(8,128)S(1)} %copy-done.1), custom_call_target="tpu_custom_call" | custom-call | tf_op jit(solution)/shard_map/sums/pallas_call | solution.py:105
  10.1 1.7 %collective-permute-start.2 = (f32[512,128]{1,0:T(8,128)S(1)}, f32[512,128]{1,0:T(8,128)S(1)}, u32[]{:S(2)}, u32[]{:S(2)}) collective-permute-start(f32[512,128]{1,0:T(8,128)S(1)} %get-tuple-element.34), channel_id=1, source_target_pairs={{0,32},{1,5},{2,34},{3,7},{4,36},{5,1},{6,38},{7,3},{8,40},{9,13},... | collective-permute-start | bytes 786440 | tf_op jit(solution)/shard_map/ppermute | solution.py:317
  11.7 0.0 collective-permute-start
  11.7 0.0 copy-done.2
  11.7 0.0 copy-done.4
  11.7 0.1 centred_weight.1.refs_3_
  11.9 1.1 %collective-permute-done = f32[160,128]{1,0:T(8,128)S(1)} collective-permute-done((f32[160,128]{1,0:T(8,128)S(1)}, f32[160,128]{1,0:T(8,128)S(1)}, u32[]{:S(2)}, u32[]{:S(2)}) %collective-permute-start) | collective-permute-done | bytes 81952 | tf_op jit(solution)/shard_map/ppermute | solution.py:317
  13.1 0.9 %collective-permute-start.1 = (f32[136,128]{1,0:T(8,128)S(1)}, f32[136,128]{1,0:T(8,128)S(1)}, u32[]{:S(2)}, u32[]{:S(2)}) collective-permute-start(f32[136,128]{1,0:T(8,128)S(1)} %slice.16.refs_4_.payload_ref), channel_id=1, source_target_pairs={{0,32},{1,5},{2,34},{3,7},{4,36},{5,1},{6,38},{7,3},{8,40},{9,13},... | collective-permute-start | bytes 208904 | tf_op jit(solution)/shard_map/ppermute | solution.py:317
  13.9 2.9 %gradient_piece.4._.refs_5_ = bf16[3,24,128,128]{3,2,1,0:T(8,128)(2,1)S(1)} custom-call(bf16[8,24,128,128]{3,2,1,0:T(8,128)(2,1)S(1)} %get-tuple-element.31.refs_0_, bf16[8,24,128,128]{3,2,1,0:T(8,128)(2,1)S(1)} %get-tuple-element.32.refs_1_, s32[24,1024]{1,0:T(8,128)S(1)} %copy-done.1, bf16[256,128]{1,0:T(8,128)(2,1)S(1)} %centred_weight.1.refs_3_, ...), custom_call_target="tpu_custom_call" | custom-call | flops 905969664 | bytes 7077888 | tf_op jit(solution)/shard_map/gradient_piece/pallas_call | solution.py:254
  16.8 0.6 %collective-permute-done.1.got_ref = f32[136,128]{1,0:T(8,128)S(1)} collective-permute-done((f32[136,128]{1,0:T(8,128)S(1)}, f32[136,128]{1,0:T(8,128)S(1)}, u32[]{:S(2)}, u32[]{:S(2)}) %collective-permute-start.1) | collective-permute-done | bytes 69664 | tf_op jit(solution)/shard_map/ppermute | solution.py:317
  17.4 0.0 collective-permute-done.2.col_ref
  17.5 1.7 %collective-permute-start.3 = (f32[392,128]{1,0:T(8,128)S(1)}, f32[392,128]{1,0:T(8,128)S(1)}, u32[]{:S(2)}, u32[]{:S(2)}) collective-permute-start(f32[392,128]{1,0:T(8,128)S(1)} %get-tuple-element.36.refs_4_.payload_ref), channel_id=1, source_target_pairs={{0,4},{1,33},{2,6},{3,35},{4,0},{5,37},{6,2},{7,39},{8,12},{9,41},... | collective-permute-start | bytes 602120 | tf_op jit(solution)/shard_map/ppermute | solution.py:317
  19.1 2.6 %gradient_piece.5 = (bf16[2,24,128,128]{3,2,1,0:T(8,128)(2,1)S(1)}, bf16[24,1024,128]{2,1,0:T(8,128)(2,1)}) custom-call(bf16[8,24,128,128]{3,2,1,0:T(8,128)(2,1)S(1)} %get-tuple-element.31.refs_0_, bf16[8,24,128,128]{3,2,1,0:T(8,128)(2,1)S(1)} %get-tuple-element.32.refs_1_, s32[24,1024]{1,0:T(8,128)S(1)} %copy-done.1, ...), custom_call_target="tpu_custom_call" | custom-call | flops 603979776 | bytes 4718592 | tf_op jit(solution)/shard_map/gradient_piece/pallas_call | solution.py:254
  21.8 1.5 %collective-permute-done.3.got_ref.col_ref = f32[392,128]{1,0:T(8,128)S(1)} collective-permute-done((f32[392,128]{1,0:T(8,128)S(1)}, f32[392,128]{1,0:T(8,128)S(1)}, u32[]{:S(2)}, u32[]{:S(2)}) %collective-permute-start.3) | collective-permute-done | bytes 200736 | tf_op jit(solution)/shard_map/ppermute | solution.py:317
  23.3 2.8 %collective-permute-start.4 = (f32[264,128]{1,0:T(8,128)S(1)}, f32[264,128]{1,0:T(8,128)S(1)}, u32[]{:S(2)}, u32[]{:S(2)}) collective-permute-start(f32[264,128]{1,0:T(8,128)S(1)} %get-tuple-element.39.refs_4_.payload_ref), channel_id=1, source_target_pairs={{0,96},{1,13},{2,98},{3,15},{4,100},{5,9},{6,102},{7,11},{8,104},{... | collective-permute-start | bytes 405512 | tf_op jit(solution)/shard_map/ppermute | solution.py:317
  26.1 2.0 %gradient_piece.6 = (bf16[2,24,128,128]{3,2,1,0:T(8,128)(2,1)S(1)}, bf16[24,1024,128]{2,1,0:T(8,128)(2,1)}) custom-call(bf16[8,24,128,128]{3,2,1,0:T(8,128)(2,1)S(1)} %get-tuple-element.31.refs_0_, bf16[8,24,128,128]{3,2,1,0:T(8,128)(2,1)S(1)} %get-tuple-element.32.refs_1_, s32[24,1024]{1,0:T(8,128)S(1)} %copy-done.1, ...), custom_call_target="tpu_custom_call", output_to_operand_aliasing={{1}: (6, {})} | custom-call | flops 603979776 | bytes 4718592 | tf_op jit(solution)/shard_map/gradient_piece/pallas_call | solution.py:254
  28.1 1.5 %collective-permute-done.4.got_ref.col_ref = f32[264,128]{1,0:T(8,128)S(1)} collective-permute-done((f32[264,128]{1,0:T(8,128)S(1)}, f32[264,128]{1,0:T(8,128)S(1)}, u32[]{:S(2)}, u32[]{:S(2)}) %collective-permute-start.4) | collective-permute-done | bytes 135200 | tf_op jit(solution)/shard_map/ppermute | solution.py:317
  29.6 3.1 %collective-permute-start.5 = (f32[200,128]{1,0:T(8,128)S(1)}, f32[200,128]{1,0:T(8,128)S(1)}, u32[]{:S(2)}, u32[]{:S(2)}) collective-permute-start(f32[200,128]{1,0:T(8,128)S(1)} %get-tuple-element.43.refs_4_.payload_ref), channel_id=1, source_target_pairs={{0,12},{1,97},{2,14},{3,99},{4,8},{5,101},{6,10},{7,103},{8,4},{9,... | collective-permute-start | bytes 307208 | tf_op jit(solution)/shard_map/ppermute | solution.py:317
  32.7 2.0 %gradient_piece.7 = (bf16[1,24,128,128]{3,2,1,0:T(8,128)(2,1)S(1)}, bf16[24,1024,128]{2,1,0:T(8,128)(2,1)}) custom-call(bf16[8,24,128,128]{3,2,1,0:T(8,128)(2,1)S(1)} %get-tuple-element.31.refs_0_, bf16[8,24,128,128]{3,2,1,0:T(8,128)(2,1)S(1)} %get-tuple-element.32.refs_1_, s32[24,1024]{1,0:T(8,128)S(1)} %copy-done.1, ...), custom_call_target="tpu_custom_call", output_to_operand_aliasing={{1}: (6, {})} | custom-call | flops 301989888 | bytes 2359296 | tf_op jit(solution)/shard_map/gradient_piece/pallas_call | solution.py:254
  34.7 0.9 %collective-permute-done.5.got_ref.col_ref = f32[200,128]{1,0:T(8,128)S(1)} collective-permute-done((f32[200,128]{1,0:T(8,128)S(1)}, f32[200,128]{1,0:T(8,128)S(1)}, u32[]{:S(2)}, u32[]{:S(2)}) %collective-permute-start.5) | collective-permute-done | bytes 102432 | tf_op jit(solution)/shard_map/ppermute | solution.py:317
  35.6 0.0 slice-done
  35.7 2.0 %collective-permute-start.6 = (f32[192,128]{1,0:T(8,128)S(1)}, f32[192,128]{1,0:T(8,128)S(1)}, u32[]{:S(2)}, u32[]{:S(2)}) collective-permute-start(f32[192,128]{1,0:T(8,128)S(1)} %pad_maximum_fusion.payload_ref), channel_id=1, source_target_pairs={{0,2},{1,3},{2,0},{3,1},{4,6},{5,7},{6,4},{7,5},{8,10},{9,11},{10,... | collective-permute-start | bytes 294920 | tf_op jit(solution)/shard_map/ppermute | solution.py:317
  37.7 2.7 %collective-permute-done.6.got_ref = f32[192,128]{1,0:T(8,128)S(1)} collective-permute-done((f32[192,128]{1,0:T(8,128)S(1)}, f32[192,128]{1,0:T(8,128)S(1)}, u32[]{:S(2)}, u32[]{:S(2)}) %collective-permute-start.6) | collective-permute-done | bytes 98336 | tf_op jit(solution)/shard_map/ppermute | solution.py:317
  40.4 4.1 %collective-permute-start.7 = (f32[168,128]{1,0:T(8,128)S(1)}, f32[168,128]{1,0:T(8,128)S(1)}, u32[]{:S(2)}, u32[]{:S(2)}) collective-permute-start(f32[168,128]{1,0:T(8,128)S(1)} %get-tuple-element.50.g_ref), channel_id=1, source_target_pairs={{0,18},{1,19},{2,16},{3,17},{4,22},{5,23},{6,20},{7,21},{8,26},{9,... | collective-permute-start | bytes 258056 | tf_op jit(solution)/shard_map/ppermute | solution.py:317
  44.5 0.0 copy-done
  44.5 0.8 %fusion = f32[24,384]{1,0:T(8,128)} fusion(f32[24,128]{1,0:T(8,128)S(1)} %get-tuple-element.49, bf16[384,128]{1,0:T(8,128)(2,1)S(1)} %copy-done), kind=kOutput, calls=%fused_computation.1 | convolution fusion | flops 14155776 | bytes 147456 | tf_op jit(solution)/shard_map/rc,sc->rs/dot_general | solution.py:352
  45.3 1.6 %collective-permute-done.7.got_ref = f32[168,128]{1,0:T(8,128)S(1)} collective-permute-done((f32[168,128]{1,0:T(8,128)S(1)}, f32[168,128]{1,0:T(8,128)S(1)}, u32[]{:S(2)}, u32[]{:S(2)}) %collective-permute-start.7) | collective-permute-done | bytes 86048 | tf_op jit(solution)/shard_map/ppermute | solution.py:317
  47.0 0.0 copy-done.3
  47.0 0.9 %parameter_gradients.1 = (f32[128,128]{1,0:T(8,128)}, f32[1,128]{1,0:T(1,128)}, f32[1,128]{1,0:T(1,128)}, f32[32,384]{1,0:T(8,128)}) custom-call(f32[168,128]{1,0:T(8,128)S(1)} %get-tuple-element.50.g_ref, f32[168,128]{1,0:T(8,128)S(1)} %collective-permute-done.7.got_ref, f32[32,128]{1,0:T(8,128)S(1)} %get-tuple-element.51.keep_ref, f32[1,128]{1,0:T(1,128)S(1)} %bitcast.7, ...), custom_call_target="tpu_custom_call" | custom-call | tf_op jit(solution)/shard_map/parameter_gradients/pallas_call | solution.py:288
  (18 shorter events, 0.2 us)
Async XLA Ops:
  0.6 43.9 %copy-start = (bf16[384,128]{1,0:T(8,128)(2,1)S(1)}, bf16[384,128]{1,0:T(8,128)(2,1)}, u32[]{:S(2)}) copy-start(bf16[384,128]{1,0:T(8,128)(2,1)} %param.14) | copy-start | bytes 294916
  0.6 0.9 %copy-start.1 = (s32[24,1024]{1,0:T(8,128)S(1)}, s32[24,1024]{1,0:T(8,128)}, u32[]{:S(2)}) copy-start(s32[24,1024]{1,0:T(8,128)} %refs_2_.7) | copy-start | bytes 294916
  1.6 10.2 %copy-start.2 = (bf16[128,128]{1,0:T(8,128)(2,1)S(1)}, bf16[128,128]{1,0:T(8,128)(2,1)}, u32[]{:S(2)}) copy-start(bf16[128,128]{1,0:T(8,128)(2,1)} %w_ref.3) | copy-start | bytes 98308
  1.6 10.2 %copy-start.4 = (f32[128]{0:T(128)S(1)}, f32[128]{0:T(128)}, u32[]{:S(2)}) copy-start(f32[128]{0:T(128)} %param.11) | copy-start | bytes 1540
  10.1 7.4 %collective-permute-start.2 = (f32[512,128]{1,0:T(8,128)S(1)}, f32[512,128]{1,0:T(8,128)S(1)}, u32[]{:S(2)}, u32[]{:S(2)}) collective-permute-start(f32[512,128]{1,0:T(8,128)S(1)} %get-tuple-element.34), channel_id=1, source_target_pairs={{0,32},{1,5},{2,34},{3,7},{4,36},{5,1},{6,38},{7,3},{8,40},{9,13},... | collective-permute-start | bytes 786440 | tf_op jit(solution)/shard_map/ppermute | solution.py:317
  11.7 1.3 %collective-permute-start = (f32[160,128]{1,0:T(8,128)S(1)}, f32[160,128]{1,0:T(8,128)S(1)}, u32[]{:S(2)}, u32[]{:S(2)}) collective-permute-start(f32[160,128]{1,0:T(8,128)S(1)} %get-tuple-element.33._), channel_id=1, source_target_pairs={{0,1},{1,0},{2,3},{3,2},{4,5},{5,4},{6,7},{7,6},{8,9},{9,8},{10,11... | collective-permute-start | bytes 245768 | tf_op jit(solution)/shard_map/ppermute | solution.py:317
  13.0 19.7 %copy-start.6 = (f32[160,128]{1,0:T(8,128)}, f32[160,128]{1,0:T(8,128)S(1)}, u32[]{:S(2)}) copy-start(f32[160,128]{1,0:T(8,128)S(1)} %add.3) | copy-start | bytes 245764
  13.1 4.4 %collective-permute-start.1 = (f32[136,128]{1,0:T(8,128)S(1)}, f32[136,128]{1,0:T(8,128)S(1)}, u32[]{:S(2)}, u32[]{:S(2)}) collective-permute-start(f32[136,128]{1,0:T(8,128)S(1)} %slice.16.refs_4_.payload_ref), channel_id=1, source_target_pairs={{0,32},{1,5},{2,34},{3,7},{4,36},{5,1},{6,38},{7,3},{8,40},{9,13},... | collective-permute-start | bytes 208904 | tf_op jit(solution)/shard_map/ppermute | solution.py:317
  17.5 5.8 %collective-permute-start.3 = (f32[392,128]{1,0:T(8,128)S(1)}, f32[392,128]{1,0:T(8,128)S(1)}, u32[]{:S(2)}, u32[]{:S(2)}) collective-permute-start(f32[392,128]{1,0:T(8,128)S(1)} %get-tuple-element.36.refs_4_.payload_ref), channel_id=1, source_target_pairs={{0,4},{1,33},{2,6},{3,35},{4,0},{5,37},{6,2},{7,39},{8,12},{9,41},... | collective-permute-start | bytes 602120 | tf_op jit(solution)/shard_map/ppermute | solution.py:317
  23.3 6.3 %collective-permute-start.4 = (f32[264,128]{1,0:T(8,128)S(1)}, f32[264,128]{1,0:T(8,128)S(1)}, u32[]{:S(2)}, u32[]{:S(2)}) collective-permute-start(f32[264,128]{1,0:T(8,128)S(1)} %get-tuple-element.39.refs_4_.payload_ref), channel_id=1, source_target_pairs={{0,96},{1,13},{2,98},{3,15},{4,100},{5,9},{6,102},{7,11},{8,104},{... | collective-permute-start | bytes 405512 | tf_op jit(solution)/shard_map/ppermute | solution.py:317
  29.6 6.0 %collective-permute-start.5 = (f32[200,128]{1,0:T(8,128)S(1)}, f32[200,128]{1,0:T(8,128)S(1)}, u32[]{:S(2)}, u32[]{:S(2)}) collective-permute-start(f32[200,128]{1,0:T(8,128)S(1)} %get-tuple-element.43.refs_4_.payload_ref), channel_id=1, source_target_pairs={{0,12},{1,97},{2,14},{3,99},{4,8},{5,101},{6,10},{7,103},{8,4},{9,... | collective-permute-start | bytes 307208 | tf_op jit(solution)/shard_map/ppermute | solution.py:317
  32.7 2.9 %slice-start = ((f32[160,128]{1,0:T(8,128)}), f32[24,128]{1,0:T(8,128)S(1)}, s32[]{:S(2)}) async-start(f32[160,128]{1,0:T(8,128)} %copy-done.6), calls=%async_computation | async-start | bytes 24576 | tf_op jit(solution)/shard_map/slice | solution.py:341
  32.7 14.2 %copy-start.3 = (bf16[384,128]{1,0:T(8,128)(2,1)S(1)}, bf16[384,128]{1,0:T(8,128)(2,1)}, u32[]{:S(2)}) copy-start(bf16[384,128]{1,0:T(8,128)(2,1)} %right_ref.1) | copy-start | bytes 294916
  32.7 14.2 %copy-start.5 = (f32[128]{0:T(128)S(1)}, f32[128]{0:T(128)}, u32[]{:S(2)}) copy-start(f32[128]{0:T(128)} %param.12) | copy-start | bytes 1540
  35.7 4.7 %collective-permute-start.6 = (f32[192,128]{1,0:T(8,128)S(1)}, f32[192,128]{1,0:T(8,128)S(1)}, u32[]{:S(2)}, u32[]{:S(2)}) collective-permute-start(f32[192,128]{1,0:T(8,128)S(1)} %pad_maximum_fusion.payload_ref), channel_id=1, source_target_pairs={{0,2},{1,3},{2,0},{3,1},{4,6},{5,7},{6,4},{7,5},{8,10},{9,11},{10,... | collective-permute-start | bytes 294920 | tf_op jit(solution)/shard_map/ppermute | solution.py:317
  40.4 6.6 %collective-permute-start.7 = (f32[168,128]{1,0:T(8,128)S(1)}, f32[168,128]{1,0:T(8,128)S(1)}, u32[]{:S(2)}, u32[]{:S(2)}) collective-permute-start(f32[168,128]{1,0:T(8,128)S(1)} %get-tuple-element.50.g_ref), channel_id=1, source_target_pairs={{0,18},{1,19},{2,16},{3,17},{4,22},{5,23},{6,20},{7,21},{8,26},{9,... | collective-permute-start | bytes 258056 | tf_op jit(solution)/shard_map/ppermute | solution.py:317

commit v4 on v3

--- a/solution.py
+++ b/solution.py
@@ -17,7 +17,7 @@
 
 
 def sums_kernel(
-    x_hbm, cot_hbm, mask_hbm, g_ref, send_ref, keep_ref, xv, cv, mask_ref, mf, mv, cc, sems, mask_sem
+    x_hbm, cot_hbm, mask_hbm, g_ref, send_ref, keep_ref, xv, cv, mf, mask_ref, mv, cc, sems, mask_sem
 ):
     rows, n, c = x_hbm.shape
     chunks = n // COLS
@@ -34,10 +34,13 @@
 
     mask_copy = pltpu.make_async_copy(mask_hbm, mask_ref, mask_sem)
     mask_copy.start()
-    for j in range(chunks):
+    for j in range(1):
         for copy in copies(j):
             copy.start()
     mask_copy.wait()
+    for j in range(1, chunks):
+        for copy in copies(j):
+            copy.start()
     lane = lax.broadcasted_iota(jnp.int32, (bands, COLS), 1) // SUB
     for j in range(chunks):
         mf[j * rows:(j + 1) * rows, :] = mask_ref[:, j * COLS:(j + 1) * COLS].astype(jnp.float32)
@@ -105,17 +108,17 @@
     return pl.pallas_call(
         sums_kernel,
         in_specs=[hbm, hbm, hbm],
-        out_specs=[vm] * 5,
+        out_specs=[vm] * 6,
         out_shape=[
             jax.ShapeDtypeStruct((c + 8 + rows, c), jnp.float32),
             jax.ShapeDtypeStruct((n // 2, c), jnp.float32),
             jax.ShapeDtypeStruct((n // 2, c), jnp.float32),
             chunks,
             chunks,
+            jax.ShapeDtypeStruct((rows * (n // COLS), COLS), jnp.float32),
         ],
         scratch_shapes=[
             pltpu.VMEM((rows, n), jnp.int32),
-            pltpu.VMEM((rows * (n // COLS), COLS), jnp.float32),
             pltpu.VMEM((COLS // SUB, n // COLS, 8, COLS), jnp.float32),
             pltpu.VMEM((n, c), jnp.float32),
             pltpu.SemaphoreType.DMA((2, n // COLS)),
@@ -213,7 +216,7 @@
         both = lax.dot_general(wt_ref[...], cv[j].reshape(p, c), NT, preferred_element_type=jnp.float32)
         dc = both[:c] + both[c:]
         mask = jnp.concatenate(
-            [mask_ref[i:i + 1, j * COLS:(j + 1) * COLS].astype(jnp.float32) for i in range(rows)], axis=1
+            [mask_ref[j * rows + i:j * rows + i + 1, :] for i in range(rows)], axis=1
         )
         xt = xv[j].reshape(p, c).T.astype(jnp.float32)
         xc = xt - jnp.sum(xt, axis=0, keepdims=True) * (1.0 / c)
@@ -333,7 +336,7 @@
     pairs = rows * lax.axis_size("row") * n * lax.axis_size("col")
     scale = 1.0 / float(pairs) ** 0.5
     parts = c + 8
-    sums_here, send, keep, xv, cv = sums(pair_act, pair_cot, pair_mask)
+    sums_here, send, keep, xv, cv, masks = sums(pair_act, pair_cot, pltpu.with_memory_space_constraint(pair_mask, pltpu.HBM))
     wt = centred_weight(gain, w, sums_here)
     prev = out = None
     col = exchange(send, *ORDER[0])
@@ -342,7 +345,7 @@
     for step, (move, other) in enumerate(ORDER):
         got = exchange(payload, move, other)
         first, count = PIECES[step]
-        prev, out = piece(xv, cv, pair_mask, wt, payload, prev, out, first=first, count=count)
+        prev, out = piece(xv, cv, masks, wt, payload, prev, out, first=first, count=count)
         payload, keep = halve(payload, got, got if step else col, keep, prev, parts)
     payload = jnp.concatenate([payload[:parts], row_part, payload[parts:]], axis=0)
     got = exchange(payload, ("z", 1))

time: 48 us -> 47.4 us (0.987)
  local copies, waits for them, and re-layouts: 0.97 us -> 0.05 us
    unnamed x14 -> x12, local copies, waits for them, and re-layouts: 0.95 us -> 0.03 us
where the time goes in v4:
time: 47.4 us; the launch traced here: 47.3 us
  Pallas kernels  19.5 us (41%)
  starting transfers between devices  16.1 us (34%)
  waiting for transfers between devices  9.94 us (21%)
  matrix products  0.84 us (2%)
  between operations  0.79 us (2%)
    ppermute x8, starting transfers between devices, exchange(): return lax.ppermute(value, ('row', 'col'), pairs)  16.1 us
    ppermute x8, waiting for transfers between devices, exchange(): return lax.ppermute(value, ('row', 'col'), pairs)  9.94 us
    pallas_call x4, Pallas kernels, piece(): pl.pallas_call(functools.partial(piece_kernel, first=first, count=count,...  9.57 us
    pallas_call x1, Pallas kernels, sums(): pl.pallas_call(sums_kernel, in_specs=[hbm, hbm, hbm], out_specs=[vm] * 6,...  8.78 us
    pallas_call x1, Pallas kernels, tail(): pl.pallas_call(functools.partial(tail_kernel, scale=scale), in_specs=[vm]...  0.95 us
  transfers between devices with their start and end apart: 8, of which 7 were waited for; matrix products, arithmetic and copies ran while one was open for 2% of the time, Pallas kernels for 20%

profile of v4, /device:TPU:0, one launch (start us, length us, event | category | flops | bytes accessed | tf_op | source)
XLA Modules:
  0.0 47.3 jit_solution(4961561046846031559)
XLA Ops:
  0.6 0.0 copy-start
  0.6 0.0 copy-start.1
  0.7 0.0 copy-start.3
  0.7 8.8 %sums.1 = (f32[160,128]{1,0:T(8,128)S(1)}, f32[512,128]{1,0:T(8,128)S(1)}, f32[512,128]{1,0:T(8,128)S(1)}, bf16[8,24,128,128]{3,2,1,0:T(8,128)(2,1)S(1)}, bf16[8...) custom-call(bf16[24,1024,128]{2,1,0:T(8,128)(2,1)} %x_hbm.1, bf16[24,1024,128]{2,1,0:T(8,128)(2,1)} %cot_hbm.1, ...), custom_call_target="tpu_custom_call" | custom-call | tf_op jit(solution)/shard_map/sums/pallas_call | solution.py:108
  9.5 1.7 %collective-permute-start.2 = (f32[512,128]{1,0:T(8,128)S(1)}, f32[512,128]{1,0:T(8,128)S(1)}, u32[]{:S(2)}, u32[]{:S(2)}) collective-permute-start(f32[512,128]{1,0:T(8,128)S(1)} %get-tuple-element.36), channel_id=1, source_target_pairs={{0,32},{1,5},{2,34},{3,7},{4,36},{5,1},{6,38},{7,3},{8,40},{9,13},... | collective-permute-start | bytes 786440 | tf_op jit(solution)/shard_map/ppermute | solution.py:320
  11.1 0.0 collective-permute-start
  11.1 0.0 copy-done.1
  11.1 0.0 copy-done.3
  11.1 0.1 centred_weight.1.refs_3_
  11.2 1.1 %collective-permute-done = f32[160,128]{1,0:T(8,128)S(1)} collective-permute-done((f32[160,128]{1,0:T(8,128)S(1)}, f32[160,128]{1,0:T(8,128)S(1)}, u32[]{:S(2)}, u32[]{:S(2)}) %collective-permute-start) | collective-permute-done | bytes 81952 | tf_op jit(solution)/shard_map/ppermute | solution.py:320
  12.4 0.0 copy-start.5
  12.4 0.8 %collective-permute-start.1 = (f32[136,128]{1,0:T(8,128)S(1)}, f32[136,128]{1,0:T(8,128)S(1)}, u32[]{:S(2)}, u32[]{:S(2)}) collective-permute-start(f32[136,128]{1,0:T(8,128)S(1)} %slice.16.refs_4_.payload_ref), channel_id=1, source_target_pairs={{0,32},{1,5},{2,34},{3,7},{4,36},{5,1},{6,38},{7,3},{8,40},{9,13},... | collective-permute-start | bytes 208904 | tf_op jit(solution)/shard_map/ppermute | solution.py:320
  13.3 2.9 %gradient_piece.4._.refs_5_ = bf16[3,24,128,128]{3,2,1,0:T(8,128)(2,1)S(1)} custom-call(bf16[8,24,128,128]{3,2,1,0:T(8,128)(2,1)S(1)} %get-tuple-element.32.refs_0_, bf16[8,24,128,128]{3,2,1,0:T(8,128)(2,1)S(1)} %get-tuple-element.33.refs_1_, f32[192,128]{1,0:T(8,128)S(1)} %get-tuple-element.34.refs_2_, bf16[256,128]{1,0:T(8,128)(2,1)S(1)} %centred_weight.1.refs_3_, ...), custom_call_target="tpu_custom_call" | custom-call | flops 905969664 | bytes 7077888 | tf_op jit(solution)/shard_map/gradient_piece/pallas_call | solution.py:257
  16.2 0.7 %collective-permute-done.1.got_ref = f32[136,128]{1,0:T(8,128)S(1)} collective-permute-done((f32[136,128]{1,0:T(8,128)S(1)}, f32[136,128]{1,0:T(8,128)S(1)}, u32[]{:S(2)}, u32[]{:S(2)}) %collective-permute-start.1) | collective-permute-done | bytes 69664 | tf_op jit(solution)/shard_map/ppermute | solution.py:320
  16.8 0.0 collective-permute-done.2.col_ref
  16.9 1.7 %collective-permute-start.3 = (f32[392,128]{1,0:T(8,128)S(1)}, f32[392,128]{1,0:T(8,128)S(1)}, u32[]{:S(2)}, u32[]{:S(2)}) collective-permute-start(f32[392,128]{1,0:T(8,128)S(1)} %get-tuple-element.38.refs_4_.payload_ref), channel_id=1, source_target_pairs={{0,4},{1,33},{2,6},{3,35},{4,0},{5,37},{6,2},{7,39},{8,12},{9,41},... | collective-permute-start | bytes 602120 | tf_op jit(solution)/shard_map/ppermute | solution.py:320
  18.5 2.6 %gradient_piece.5 = (bf16[2,24,128,128]{3,2,1,0:T(8,128)(2,1)S(1)}, bf16[24,1024,128]{2,1,0:T(8,128)(2,1)}) custom-call(bf16[8,24,128,128]{3,2,1,0:T(8,128)(2,1)S(1)} %get-tuple-element.32.refs_0_, bf16[8,24,128,128]{3,2,1,0:T(8,128)(2,1)S(1)} %get-tuple-element.33.refs_1_, f32[192,128]{1,0:T(8,128)S(1)} %get-tuple-element.34.refs_2_, ...), custom_call_target="tpu_custom_call" | custom-call | flops 603979776 | bytes 4718592 | tf_op jit(solution)/shard_map/gradient_piece/pallas_call | solution.py:257
  21.1 1.5 %collective-permute-done.3.got_ref.col_ref = f32[392,128]{1,0:T(8,128)S(1)} collective-permute-done((f32[392,128]{1,0:T(8,128)S(1)}, f32[392,128]{1,0:T(8,128)S(1)}, u32[]{:S(2)}, u32[]{:S(2)}) %collective-permute-start.3) | collective-permute-done | bytes 200736 | tf_op jit(solution)/shard_map/ppermute | solution.py:320
  22.7 2.8 %collective-permute-start.4 = (f32[264,128]{1,0:T(8,128)S(1)}, f32[264,128]{1,0:T(8,128)S(1)}, u32[]{:S(2)}, u32[]{:S(2)}) collective-permute-start(f32[264,128]{1,0:T(8,128)S(1)} %get-tuple-element.41.refs_4_.payload_ref), channel_id=1, source_target_pairs={{0,96},{1,13},{2,98},{3,15},{4,100},{5,9},{6,102},{7,11},{8,104},{... | collective-permute-start | bytes 405512 | tf_op jit(solution)/shard_map/ppermute | solution.py:320
  25.4 1.9 %gradient_piece.6 = (bf16[2,24,128,128]{3,2,1,0:T(8,128)(2,1)S(1)}, bf16[24,1024,128]{2,1,0:T(8,128)(2,1)}) custom-call(bf16[8,24,128,128]{3,2,1,0:T(8,128)(2,1)S(1)} %get-tuple-element.32.refs_0_, bf16[8,24,128,128]{3,2,1,0:T(8,128)(2,1)S(1)} %get-tuple-element.33.refs_1_, ...), custom_call_target="tpu_custom_call", output_to_operand_aliasing={{1}: (6, {})} | custom-call | flops 603979776 | bytes 4718592 | tf_op jit(solution)/shard_map/gradient_piece/pallas_call | solution.py:257
  27.4 1.6 %collective-permute-done.4.got_ref.col_ref = f32[264,128]{1,0:T(8,128)S(1)} collective-permute-done((f32[264,128]{1,0:T(8,128)S(1)}, f32[264,128]{1,0:T(8,128)S(1)}, u32[]{:S(2)}, u32[]{:S(2)}) %collective-permute-start.4) | collective-permute-done | bytes 135200 | tf_op jit(solution)/shard_map/ppermute | solution.py:320
  29.0 3.1 %collective-permute-start.5 = (f32[200,128]{1,0:T(8,128)S(1)}, f32[200,128]{1,0:T(8,128)S(1)}, u32[]{:S(2)}, u32[]{:S(2)}) collective-permute-start(f32[200,128]{1,0:T(8,128)S(1)} %get-tuple-element.45.refs_4_.payload_ref), channel_id=1, source_target_pairs={{0,12},{1,97},{2,14},{3,99},{4,8},{5,101},{6,10},{7,103},{8,4},{9,... | collective-permute-start | bytes 307208 | tf_op jit(solution)/shard_map/ppermute | solution.py:320
  32.1 2.1 %gradient_piece.7 = (bf16[1,24,128,128]{3,2,1,0:T(8,128)(2,1)S(1)}, bf16[24,1024,128]{2,1,0:T(8,128)(2,1)}) custom-call(bf16[8,24,128,128]{3,2,1,0:T(8,128)(2,1)S(1)} %get-tuple-element.32.refs_0_, bf16[8,24,128,128]{3,2,1,0:T(8,128)(2,1)S(1)} %get-tuple-element.33.refs_1_, ...), custom_call_target="tpu_custom_call", output_to_operand_aliasing={{1}: (6, {})} | custom-call | flops 301989888 | bytes 2359296 | tf_op jit(solution)/shard_map/gradient_piece/pallas_call | solution.py:257
  34.3 0.7 %collective-permute-done.5.got_ref.col_ref = f32[200,128]{1,0:T(8,128)S(1)} collective-permute-done((f32[200,128]{1,0:T(8,128)S(1)}, f32[200,128]{1,0:T(8,128)S(1)}, u32[]{:S(2)}, u32[]{:S(2)}) %collective-permute-start.5) | collective-permute-done | bytes 102432 | tf_op jit(solution)/shard_map/ppermute | solution.py:320
  35.0 0.0 slice-done
  35.0 2.0 %collective-permute-start.6 = (f32[192,128]{1,0:T(8,128)S(1)}, f32[192,128]{1,0:T(8,128)S(1)}, u32[]{:S(2)}, u32[]{:S(2)}) collective-permute-start(f32[192,128]{1,0:T(8,128)S(1)} %pad_maximum_fusion.payload_ref), channel_id=1, source_target_pairs={{0,2},{1,3},{2,0},{3,1},{4,6},{5,7},{6,4},{7,5},{8,10},{9,11},{10,... | collective-permute-start | bytes 294920 | tf_op jit(solution)/shard_map/ppermute | solution.py:320
  37.0 2.7 %collective-permute-done.6.got_ref = f32[192,128]{1,0:T(8,128)S(1)} collective-permute-done((f32[192,128]{1,0:T(8,128)S(1)}, f32[192,128]{1,0:T(8,128)S(1)}, u32[]{:S(2)}, u32[]{:S(2)}) %collective-permute-start.6) | collective-permute-done | bytes 98336 | tf_op jit(solution)/shard_map/ppermute | solution.py:320
  39.7 4.1 %collective-permute-start.7 = (f32[168,128]{1,0:T(8,128)S(1)}, f32[168,128]{1,0:T(8,128)S(1)}, u32[]{:S(2)}, u32[]{:S(2)}) collective-permute-start(f32[168,128]{1,0:T(8,128)S(1)} %get-tuple-element.52.g_ref), channel_id=1, source_target_pairs={{0,18},{1,19},{2,16},{3,17},{4,22},{5,23},{6,20},{7,21},{8,26},{9,... | collective-permute-start | bytes 258056 | tf_op jit(solution)/shard_map/ppermute | solution.py:320
  43.8 0.8 %fusion = f32[24,384]{1,0:T(8,128)} fusion(f32[24,128]{1,0:T(8,128)S(1)} %get-tuple-element.51, bf16[384,128]{1,0:T(8,128)(2,1)S(1)} %copy-done), kind=kOutput, calls=%fused_computation.1 | convolution fusion | flops 14155776 | bytes 147456 | tf_op jit(solution)/shard_map/rc,sc->rs/dot_general | solution.py:355
  44.7 1.6 %collective-permute-done.7.got_ref = f32[168,128]{1,0:T(8,128)S(1)} collective-permute-done((f32[168,128]{1,0:T(8,128)S(1)}, f32[168,128]{1,0:T(8,128)S(1)}, u32[]{:S(2)}, u32[]{:S(2)}) %collective-permute-start.7) | collective-permute-done | bytes 86048 | tf_op jit(solution)/shard_map/ppermute | solution.py:320
  46.3 0.0 copy-done.4
  46.3 0.9 %parameter_gradients.1 = (f32[128,128]{1,0:T(8,128)}, f32[1,128]{1,0:T(1,128)}, f32[1,128]{1,0:T(1,128)}, f32[32,384]{1,0:T(8,128)}) custom-call(f32[168,128]{1,0:T(8,128)S(1)} %get-tuple-element.52.g_ref, f32[168,128]{1,0:T(8,128)S(1)} %collective-permute-done.7.got_ref, f32[32,128]{1,0:T(8,128)S(1)} %get-tuple-element.53.keep_ref, f32[1,128]{1,0:T(1,128)S(1)} %bitcast.7, ...), custom_call_target="tpu_custom_call" | custom-call | tf_op jit(solution)/shard_map/parameter_gradients/pallas_call | solution.py:291
  (16 shorter events, 0.2 us)
Async XLA Ops:
  0.6 43.2 %copy-start = (bf16[384,128]{1,0:T(8,128)(2,1)S(1)}, bf16[384,128]{1,0:T(8,128)(2,1)}, u32[]{:S(2)}) copy-start(bf16[384,128]{1,0:T(8,128)(2,1)} %param.14) | copy-start | bytes 294916
  0.6 10.5 %copy-start.1 = (bf16[128,128]{1,0:T(8,128)(2,1)S(1)}, bf16[128,128]{1,0:T(8,128)(2,1)}, u32[]{:S(2)}) copy-start(bf16[128,128]{1,0:T(8,128)(2,1)} %w_ref.3) | copy-start | bytes 98308
  0.7 10.5 %copy-start.3 = (f32[128]{0:T(128)S(1)}, f32[128]{0:T(128)}, u32[]{:S(2)}) copy-start(f32[128]{0:T(128)} %param.11) | copy-start | bytes 1540
  9.5 7.4 %collective-permute-start.2 = (f32[512,128]{1,0:T(8,128)S(1)}, f32[512,128]{1,0:T(8,128)S(1)}, u32[]{:S(2)}, u32[]{:S(2)}) collective-permute-start(f32[512,128]{1,0:T(8,128)S(1)} %get-tuple-element.36), channel_id=1, source_target_pairs={{0,32},{1,5},{2,34},{3,7},{4,36},{5,1},{6,38},{7,3},{8,40},{9,13},... | collective-permute-start | bytes 786440 | tf_op jit(solution)/shard_map/ppermute | solution.py:320
  11.1 1.3 %collective-permute-start = (f32[160,128]{1,0:T(8,128)S(1)}, f32[160,128]{1,0:T(8,128)S(1)}, u32[]{:S(2)}, u32[]{:S(2)}) collective-permute-start(f32[160,128]{1,0:T(8,128)S(1)} %get-tuple-element.35._), channel_id=1, source_target_pairs={{0,1},{1,0},{2,3},{3,2},{4,5},{5,4},{6,7},{7,6},{8,9},{9,8},{10,11... | collective-permute-start | bytes 245768 | tf_op jit(solution)/shard_map/ppermute | solution.py:320
  12.4 19.7 %copy-start.5 = (f32[160,128]{1,0:T(8,128)}, f32[160,128]{1,0:T(8,128)S(1)}, u32[]{:S(2)}) copy-start(f32[160,128]{1,0:T(8,128)S(1)} %add.3) | copy-start | bytes 245764
  12.4 4.4 %collective-permute-start.1 = (f32[136,128]{1,0:T(8,128)S(1)}, f32[136,128]{1,0:T(8,128)S(1)}, u32[]{:S(2)}, u32[]{:S(2)}) collective-permute-start(f32[136,128]{1,0:T(8,128)S(1)} %slice.16.refs_4_.payload_ref), channel_id=1, source_target_pairs={{0,32},{1,5},{2,34},{3,7},{4,36},{5,1},{6,38},{7,3},{8,40},{9,13},... | collective-permute-start | bytes 208904 | tf_op jit(solution)/shard_map/ppermute | solution.py:320
  16.9 5.8 %collective-permute-start.3 = (f32[392,128]{1,0:T(8,128)S(1)}, f32[392,128]{1,0:T(8,128)S(1)}, u32[]{:S(2)}, u32[]{:S(2)}) collective-permute-start(f32[392,128]{1,0:T(8,128)S(1)} %get-tuple-element.38.refs_4_.payload_ref), channel_id=1, source_target_pairs={{0,4},{1,33},{2,6},{3,35},{4,0},{5,37},{6,2},{7,39},{8,12},{9,41},... | collective-permute-start | bytes 602120 | tf_op jit(solution)/shard_map/ppermute | solution.py:320
  22.7 6.3 %collective-permute-start.4 = (f32[264,128]{1,0:T(8,128)S(1)}, f32[264,128]{1,0:T(8,128)S(1)}, u32[]{:S(2)}, u32[]{:S(2)}) collective-permute-start(f32[264,128]{1,0:T(8,128)S(1)} %get-tuple-element.41.refs_4_.payload_ref), channel_id=1, source_target_pairs={{0,96},{1,13},{2,98},{3,15},{4,100},{5,9},{6,102},{7,11},{8,104},{... | collective-permute-start | bytes 405512 | tf_op jit(solution)/shard_map/ppermute | solution.py:320
  29.0 6.0 %collective-permute-start.5 = (f32[200,128]{1,0:T(8,128)S(1)}, f32[200,128]{1,0:T(8,128)S(1)}, u32[]{:S(2)}, u32[]{:S(2)}) collective-permute-start(f32[200,128]{1,0:T(8,128)S(1)} %get-tuple-element.45.refs_4_.payload_ref), channel_id=1, source_target_pairs={{0,12},{1,97},{2,14},{3,99},{4,8},{5,101},{6,10},{7,103},{8,4},{9,... | collective-permute-start | bytes 307208 | tf_op jit(solution)/shard_map/ppermute | solution.py:320
  32.1 2.9 %slice-start = ((f32[160,128]{1,0:T(8,128)}), f32[24,128]{1,0:T(8,128)S(1)}, s32[]{:S(2)}) async-start(f32[160,128]{1,0:T(8,128)} %copy-done.5), calls=%async_computation | async-start | bytes 24576 | tf_op jit(solution)/shard_map/slice | solution.py:344
  32.1 14.2 %copy-start.2 = (bf16[384,128]{1,0:T(8,128)(2,1)S(1)}, bf16[384,128]{1,0:T(8,128)(2,1)}, u32[]{:S(2)}) copy-start(bf16[384,128]{1,0:T(8,128)(2,1)} %right_ref.1) | copy-start | bytes 294916
  32.1 14.2 %copy-start.4 = (f32[128]{0:T(128)S(1)}, f32[128]{0:T(128)}, u32[]{:S(2)}) copy-start(f32[128]{0:T(128)} %param.12) | copy-start | bytes 1540
  35.0 4.7 %collective-permute-start.6 = (f32[192,128]{1,0:T(8,128)S(1)}, f32[192,128]{1,0:T(8,128)S(1)}, u32[]{:S(2)}, u32[]{:S(2)}) collective-permute-start(f32[192,128]{1,0:T(8,128)S(1)} %pad_maximum_fusion.payload_ref), channel_id=1, source_target_pairs={{0,2},{1,3},{2,0},{3,1},{4,6},{5,7},{6,4},{7,5},{8,10},{9,11},{10,... | collective-permute-start | bytes 294920 | tf_op jit(solution)/shard_map/ppermute | solution.py:320
  39.7 6.6 %collective-permute-start.7 = (f32[168,128]{1,0:T(8,128)S(1)}, f32[168,128]{1,0:T(8,128)S(1)}, u32[]{:S(2)}, u32[]{:S(2)}) collective-permute-start(f32[168,128]{1,0:T(8,128)S(1)} %get-tuple-element.52.g_ref), channel_id=1, source_target_pairs={{0,18},{1,19},{2,16},{3,17},{4,22},{5,23},{6,20},{7,21},{8,26},{9,... | collective-permute-start | bytes 258056 | tf_op jit(solution)/shard_map/ppermute | solution.py:320
